TPU v7x, 512 devices: a whole 4x4x16 slice. The times are simulated.
512 devices in a mesh: panel: 2 (over y_lo), lat: 16 (over z), lon: 16 (over y_hi, x, core).
Axes of the slice: x: 4, y: 4 (y_hi: 2, y_lo: 2; y = y_hi * 2 + y_lo), z: 16, core: 2. Of those that a mesh axis runs over, the one named last changes fastest.
Arguments:
- state: float32 [2, 7, 2, 1024, 2048], P('panel', None, None, 'lat', 'lon'), may hold values from -4 to 4
- source_slot: int32 [2, 16, 16, 768], P('panel', 'lat', 'lon'), may hold values from 0 to 12287, as said below
- donor_cell: int32 [2, 16, 16, 48], P('panel', 'lat', 'lon'), may hold values from 0 to 8000
- donor_frac: float32 [2, 16, 16, 2, 48], P('panel', 'lat', 'lon'), may hold values from 0 to 1
- donor_turn: float32 [2, 16, 16, 48], P('panel', 'lat', 'lon'), may hold values from -3.140625 to 3.140625
Outputs:
- new_state: float32 [2, 7, 2, 1024, 2048], P('panel', None, None, 'lat', 'lon')
Inputs may be any that keep to these rules, and one draw needn't show every extreme that they name: `source_slot`: entries name a partner panel donation (a * 16 + b) * 48 + s. For a device on an edge of its panel, the rim entries that lie on that edge name the donations that fill them; over a panel's whole border every donation of the partner panel is named exactly once. Other entries are unused.
All inputs are finite; a program needn't handle non-finite values.
Results may differ from a plain program's by a relative error of at most 0.00002.
Values sent between devices are 32-bit elements; how exact they have to be, the bound alone decides.
A program may use at most 64 MiB of HBM per device.

v0:
```python
import jax
import jax.numpy as jnp
from jax import lax
from jax.sharding import PartitionSpec as P

viscosity = 0.05
resistivity = 0.05
diffusivity = 0.05
buoyancy = 0.5
time_step = 0.25


def partner_2(block, axis, apart):
    count = lax.axis_size(axis)
    route = []
    for low in range(count):
        high = low | 1 << apart
        if high != low and high < count:
            route += [(low, high), (high, low)]
    return lax.ppermute(block, axis, route)


def with_halo(value, sides, width):
    for axis, dim in sides:
        size, length = (lax.axis_size(axis), value.shape[dim])
        up = [(i, (i + 1) % size) for i in range(size - 1)]
        down = [(j, i) for i, j in up]
        last = lax.slice_in_dim(value, length - width, length, axis=dim)
        initial = lax.slice_in_dim(value, 0, width, axis=dim)
        before = lax.ppermute(last, axis, up)
        after = lax.ppermute(initial, axis, down)
        value = jnp.concatenate([before, value, after], axis=dim)
    return value


def rate(ext):
    height = ext.shape[2] - 4
    width = ext.shape[3] - 4

    def lat_at(k):
        return ext[:, :, 2 + k : 2 + k + height, 2 : 2 + width]

    def lon_at(k):
        return ext[:, :, 2 : 2 + height, 2 + k : 2 + k + width]

    middle = lat_at(0)
    d_lat = (8.0 * (lat_at(1) - lat_at(-1)) - (lat_at(2) - lat_at(-2))) / 12.0
    d_lon = (8.0 * (lon_at(1) - lon_at(-1)) - (lon_at(2) - lon_at(-2))) / 12.0
    padded = jnp.pad(middle, ((0, 0), (1, 1), (0, 0), (0, 0)))
    lap = lat_at(1) + lat_at(-1) + lon_at(1) + lon_at(-1) - 4.0 * middle
    lap = lap + padded[:, 2:] + padded[:, :-2] - 2.0 * middle
    adv_u = middle[1:2] * d_lat + middle[2:3] * d_lon
    adv_b = middle[4:5] * d_lat + middle[5:6] * d_lon
    moment = -adv_u[0:3] + adv_b[3:6] + viscosity * lap[0:3]
    induct = adv_b[0:3] - adv_u[3:6] + resistivity * lap[3:6]
    heat = -adv_u[6:7] + diffusivity * lap[6:7]
    first = moment[0:1] + buoyancy * middle[6:7]
    return jnp.concatenate([first, moment[1:3], induct, heat], axis=0)


def rotate(values, turn):
    cosine = jnp.cos(turn)
    sine = jnp.sin(turn)
    parts = [
        values[0],
        cosine * values[1] - sine * values[2],
        sine * values[1] + cosine * values[2],
        values[3],
        cosine * values[4] - sine * values[5],
        sine * values[4] + cosine * values[5],
        values[6],
    ]
    return jnp.stack(parts)


def per_device(state, source_slot, donor_cell, donor_frac, donor_turn):
    comps = state.shape[1]
    levels = state.shape[2]
    rows = state.shape[3]
    cols = state.shape[4]
    cells = donor_cell[0, 0, 0]
    frac_t = donor_frac[0, 0, 0, 0]
    frac_p = donor_frac[0, 0, 0, 1]
    turn = donor_turn[0, 0, 0]
    slots = source_slot[0, 0, 0]
    index = cells // (cols - 1) * cols + cells % (cols - 1)
    lat_pos = lax.axis_index("lat")
    lon_pos = lax.axis_index("lon")
    lat_count = lax.axis_size("lat")
    lon_count = lax.axis_size("lon")

    def donate(field):
        flat = field.reshape(comps, levels, rows * cols)
        lower = jnp.take(flat, index, axis=2)
        lower_next = jnp.take(flat, index + 1, axis=2)
        upper = jnp.take(flat, index + cols, axis=2)
        upper_next = jnp.take(flat, index + cols + 1, axis=2)
        value = (
            (1.0 - frac_t) * (1.0 - frac_p) * lower
            + (1.0 - frac_t) * frac_p * lower_next
            + frac_t * (1.0 - frac_p) * upper
            + frac_t * frac_p * upper_next
        )
        return rotate(value, turn).reshape(comps * levels, -1)

    def receive(given):
        whole = lax.all_gather(given, ("lat", "lon"), axis=1, tiled=True)
        partner = partner_2(whole, "panel", 0)
        return jnp.take(partner, slots, axis=1)

    def extended(field):
        ext = with_halo(field, (("lat", 2), ("lon", 3)), 2)
        rim_values = receive(donate(field)).reshape(comps, levels, -1)
        top = rim_values[:, :, 0 : 2 * cols].reshape(comps, levels, 2, cols)
        bottom = rim_values[:, :, 2 * cols : 4 * cols].reshape(comps, levels, 2, cols)
        left = rim_values[:, :, 4 * cols : 4 * cols + 2 * rows].reshape(comps, levels, 2, rows)
        left = jnp.transpose(left, (0, 1, 3, 2))
        right = rim_values[:, :, 4 * cols + 2 * rows :].reshape(comps, levels, 2, rows)
        right = jnp.transpose(right, (0, 1, 3, 2))
        ext = ext.at[:, :, 0:2, 2 : 2 + cols].set(
            jnp.where(lat_pos == 0, top, ext[:, :, 0:2, 2 : 2 + cols])
        )
        ext = ext.at[:, :, rows + 2 : rows + 4, 2 : 2 + cols].set(
            jnp.where(
                lat_pos == lat_count - 1, bottom, ext[:, :, rows + 2 : rows + 4, 2 : 2 + cols]
            )
        )
        ext = ext.at[:, :, 2 : 2 + rows, 0:2].set(
            jnp.where(lon_pos == 0, left, ext[:, :, 2 : 2 + rows, 0:2])
        )
        ext = ext.at[:, :, 2 : 2 + rows, cols + 2 : cols + 4].set(
            jnp.where(lon_pos == lon_count - 1, right, ext[:, :, 2 : 2 + rows, cols + 2 : cols + 4])
        )
        return ext

    field = state[0]
    section_one = field + time_step * rate(extended(field))
    second = rate(extended(section_one))
    new_field = 0.5 * field + 0.5 * (section_one + time_step * second)
    return new_field[None]


def solution(mesh):
    in_specs = (
        P("panel", None, None, "lat", "lon"),
        P("panel", "lat", "lon", None),
        P("panel", "lat", "lon", None),
        P("panel", "lat", "lon", None, None),
        P("panel", "lat", "lon", None),
    )
    out_specs = P("panel", None, None, "lat", "lon")
    return jax.shard_map(
        per_device, mesh=mesh, in_specs=in_specs, out_specs=out_specs, check_vma=False
    )
```

profile of v0, /device:TPU:1, one launch (start us, length us, event | category | flops | bytes accessed | tf_op | source)
XLA Modules:
  0.0 928.0 jit_solution(459136195034202323)
XLA Ops:
  2.1 8.0 copy.156
  10.6 4.0 gather_fusion.2
  14.7 4.0 gather_fusion.3
  19.4 4.0 gather_fusion
  23.5 4.0 gather_fusion.1
  28.4 369.7 %all-gather = f32[256,48,14]{1,2,0:T(8,128)S(1)} all-gather(f32[1,48,14]{1,2,0:T(8,128)S(1)} %bitcast.153), channel_id=1, replica_groups=mesh['panel'=2,'lat'=16,'lon'=16] {'lat','lon'}, dimensions={0}, use_global_device_ids=true | all-gather | bytes 690816 | tf_op jit(solution)/shard_map/all_gather | solution.py:107
  411.4 2.8 collective-permute-start.3
  414.8 2.9 collective-permute-done.2
  418.5 3.6 collective-permute-done.3
  423.8 2.7 collective-permute-done.4
  426.5 4.0 copy.165
  430.5 4.6 gather_fusion.4
  438.3 5.8 scatter.26
  444.6 4.5 scatter.29
  449.1 9.3 %scatter.30 = f32[7,2,68,132]{3,2,1,0:T(8,128)S(1)} dynamic-update-slice(f32[7,2,68,132]{3,2,1,0:T(8,128)S(1)} %scatter.29, f32[7,2,64,2]{3,2,1,0:T(8,128)S(1)} %slice_select_fusion.3, s32[]{:T(128)} %constant.261.clone.1, s32[]{:T(128)} %constant.261.clone.1, s32[]{:T(128)} %constant.263.clone.1, s32[]{:T(128)} %constant.261.clone.1) | dynamic-update-slice | bytes 14340 | tf_op jit(solution)/shard_map/scatter | solution.py:128
  459.0 11.6 %scatter.31 = f32[7,2,68,132]{3,2,1,0:T(8,128)S(1)} dynamic-update-slice(f32[7,2,68,132]{3,2,1,0:T(8,128)S(1)} %scatter.30, f32[7,2,64,2]{3,2,1,0:T(8,128)S(1)} %slice_select_fusion.2, s32[]{:T(128)} %constant.261.clone.1, s32[]{:T(128)} %constant.261.clone.1, s32[]{:T(128)} %constant.263.clone.1, s32[]{:T(128)} %constant.276.clone.1) | dynamic-update-slice | bytes 14340 | tf_op jit(solution)/shard_map/scatter | solution.py:131
  472.9 8.0 copy.171
  480.8 4.1 gather_fusion.7
  485.0 4.1 gather_fusion.5
  489.1 4.1 gather_fusion.6
  493.2 4.1 gather_fusion.8
  498.0 354.9 %all-gather.1 = f32[256,48,14]{1,2,0:T(8,128)S(1)} all-gather(f32[1,48,14]{1,2,0:T(8,128)S(1)} %bitcast.154), channel_id=1, replica_groups=mesh['panel'=2,'lat'=16,'lon'=16] {'lat','lon'}, dimensions={0}, use_global_device_ids=true | all-gather | bytes 690816 | tf_op jit(solution)/shard_map/all_gather | solution.py:107
  860.8 3.4 collective-permute-done.6
  864.5 4.7 collective-permute-start.7
  871.1 4.1 collective-permute-done.7
  875.2 4.7 collective-permute-done.8
  882.4 4.0 copy.180
  886.5 4.3 gather_fusion.9
  893.3 5.8 scatter.34
  899.3 4.5 scatter.35
  904.1 9.3 %scatter.36 = f32[7,2,68,132]{3,2,1,0:T(8,128)S(1)} dynamic-update-slice(f32[7,2,68,132]{3,2,1,0:T(8,128)S(1)} %scatter.35, f32[7,2,64,2]{3,2,1,0:T(8,128)S(1)} %slice_select_fusion.1, s32[]{:T(128)} %constant.261.clone.1, s32[]{:T(128)} %constant.261.clone.1, s32[]{:T(128)} %constant.263.clone.1, s32[]{:T(128)} %constant.261.clone.1) | dynamic-update-slice | bytes 14340 | tf_op jit(solution)/shard_map/scatter | solution.py:128
  914.0 11.6 %scatter.39 = f32[7,2,68,132]{3,2,1,0:T(8,128)S(1)} dynamic-update-slice(f32[7,2,68,132]{3,2,1,0:T(8,128)S(1)} %scatter.36, f32[7,2,64,2]{3,2,1,0:T(8,128)S(1)} %slice_select_fusion, s32[]{:T(128)} %constant.261.clone.1, s32[]{:T(128)} %constant.261.clone.1, s32[]{:T(128)} %constant.263.clone.1, s32[]{:T(128)} %constant.276.clone.1) | dynamic-update-slice | bytes 14340 | tf_op jit(solution)/shard_map/scatter | solution.py:131
  (178 shorter events, 45.6 us)
Async XLA Ops:
  0.0 27.6 %copy-start.28 = (f32[1,1,1,2,48]{4,3,2,1,0:T(2,128)S(1)}, f32[1,1,1,2,48]{4,3,2,1,0:T(2,128)}, u32[]{:S(2)}) copy-start(f32[1,1,1,2,48]{4,3,2,1,0:T(2,128)} %param.28) | copy-start | bytes 1156
  0.0 27.7 %copy-start.29 = (f32[1,1,1,48]{3,2,1,0:T(1,128)S(1)}, f32[1,1,1,48]{3,2,1,0:T(1,128)}, u32[]{:S(2)}) copy-start(f32[1,1,1,48]{3,2,1,0:T(1,128)} %param.29) | copy-start | bytes 580
  0.7 27.6 %copy-start.26 = (pred[48]{0:T(512)(128)(4,1)}, pred[48]{0:T(512)(128)(4,1)S(1)}, u32[]{:S(2)}) copy-start(pred[48]{0:T(512)(128)(4,1)S(1)} %get-tuple-element.109) | copy-start | bytes 148
  0.7 27.6 %copy-start.12 = (pred[48]{0:T(512)(128)(4,1)}, pred[48]{0:T(512)(128)(4,1)S(1)}, u32[]{:S(2)}) copy-start(pred[48]{0:T(512)(128)(4,1)S(1)} %get-tuple-element.111) | copy-start | bytes 148
  0.7 27.6 %copy-start.14 = (pred[48]{0:T(512)(128)(4,1)}, pred[48]{0:T(512)(128)(4,1)S(1)}, u32[]{:S(2)}) copy-start(pred[48]{0:T(512)(128)(4,1)S(1)} %get-tuple-element.155) | copy-start | bytes 148
  0.8 27.6 %copy-start.16 = (pred[48]{0:T(512)(128)(4,1)}, pred[48]{0:T(512)(128)(4,1)S(1)}, u32[]{:S(2)}) copy-start(pred[48]{0:T(512)(128)(4,1)S(1)} %get-tuple-element.157) | copy-start | bytes 148
  2.1 400.2 %copy-start = (f32[1,7,2,64,128]{4,3,2,1,0:T(8,128)S(1)}, f32[1,7,2,64,128]{4,3,2,1,0:T(8,128)}, u32[]{:S(2)}) copy-start(f32[1,7,2,64,128]{4,3,2,1,0:T(8,128)} %param.25) | copy-start | bytes 1376260
  10.0 4.7 copy-start.8
  18.9 4.7 copy-start.10
  400.1 26.4 %collective-permute-start.4 = (f32[14,12288]{1,0:T(8,128)S(1)}, f32[14,12288]{1,0:T(8,128)S(1)}, u32[]{:S(2)}, u32[]{:S(2)}) collective-permute-start(f32[14,12288]{1,0:T(8,128)S(1)} %bitcast.151), channel_id=1, source_target_pairs={{0,256},{256,0},{1,257},{257,1},{2,258},{258,2},{3,259},{259,3},{4... | collective-permute-start | bytes 2064392 | tf_op jit(solution)/shard_map/ppermute | solution.py:20
  402.3 6.0 collective-permute-start
  403.6 4.8 collective-permute-start.1
  409.4 8.2 collective-permute-start.2
  411.4 10.7 %collective-permute-start.3 = (f32[7,2,68,2]{3,2,1,0:T(8,128)S(1)}, f32[7,2,68,2]{3,2,1,0:T(8,128)}, u32[]{:S(2)}, u32[]{:S(2)}) collective-permute-start(f32[7,2,68,2]{3,2,1,0:T(8,128)S(1)} %get-tuple-element.134), channel_id=1, source_target_pairs={{1,0},{2,1},{3,2},{4,3},{5,4},{6,5},{7,6},{8,7},{9,8},{10,9},{11,1... | collective-permute-start | bytes 22856 | tf_op jit(solution)/shard_map/ppermute | solution.py:31
  417.7 0.8 copy-start.1
  471.8 26.0 %copy-start.13 = (pred[48]{0:T(512)(128)(4,1)S(1)}, pred[48]{0:T(512)(128)(4,1)}, u32[]{:S(2)}) copy-start(pred[48]{0:T(512)(128)(4,1)} %copy-done.12) | copy-start | bytes 148
  471.8 26.0 %copy-start.15 = (pred[48]{0:T(512)(128)(4,1)S(1)}, pred[48]{0:T(512)(128)(4,1)}, u32[]{:S(2)}) copy-start(pred[48]{0:T(512)(128)(4,1)} %copy-done.14) | copy-start | bytes 148
  471.8 26.0 %copy-start.17 = (pred[48]{0:T(512)(128)(4,1)S(1)}, pred[48]{0:T(512)(128)(4,1)}, u32[]{:S(2)}) copy-start(pred[48]{0:T(512)(128)(4,1)} %copy-done.16) | copy-start | bytes 148
  471.8 26.0 %copy-start.19 = (f32[48]{0:T(128)S(1)}, f32[48]{0:T(128)}, u32[]{:S(2)}) copy-start(f32[48]{0:T(128)} %copy-done.18) | copy-start | bytes 580
  471.8 26.0 %copy-start.21 = (f32[48]{0:T(128)S(1)}, f32[48]{0:T(128)}, u32[]{:S(2)}) copy-start(f32[48]{0:T(128)} %copy-done.20) | copy-start | bytes 580
  471.8 26.0 %copy-start.23 = (f32[48]{0:T(128)S(1)}, f32[48]{0:T(128)}, u32[]{:S(2)}) copy-start(f32[48]{0:T(128)} %copy-done.22) | copy-start | bytes 580
  471.8 26.0 %copy-start.25 = (f32[48]{0:T(128)S(1)}, f32[48]{0:T(128)}, u32[]{:S(2)}) copy-start(f32[48]{0:T(128)} %copy-done.24) | copy-start | bytes 580
  471.8 26.0 %copy-start.27 = (pred[48]{0:T(512)(128)(4,1)S(1)}, pred[48]{0:T(512)(128)(4,1)}, u32[]{:S(2)}) copy-start(pred[48]{0:T(512)(128)(4,1)} %copy-done.26) | copy-start | bytes 148
  471.8 26.0 %copy-start.4 = (f32[48]{0:T(128)S(1)}, f32[48]{0:T(128)}, u32[]{:S(2)}) copy-start(f32[48]{0:T(128)} %copy-done.3) | copy-start | bytes 580
  471.9 26.0 %copy-start.6 = (f32[48]{0:T(128)S(1)}, f32[48]{0:T(128)}, u32[]{:S(2)}) copy-start(f32[48]{0:T(128)} %copy-done.5) | copy-start | bytes 580
  853.5 33.0 %copy-start.2 = (s32[1024]{0:T(1024)S(1)}, s32[1024]{0:T(1024)}, u32[]{:S(2)}) copy-start(s32[1024]{0:T(1024)} %pad_clamp_fusion) | copy-start | bytes 12292
  853.5 37.4 %copy-start.7 = (pred[768]{0:T(1024)(128)(4,1)S(1)}, pred[768]{0:T(1024)(128)(4,1)}, u32[]{:S(2)}) copy-start(pred[768]{0:T(1024)(128)(4,1)} %compare_and_fusion) | copy-start | bytes 2308
  855.8 26.6 %collective-permute-start.9 = (f32[14,12288]{1,0:T(8,128)}, f32[14,12288]{1,0:T(8,128)S(1)}, u32[]{:S(2)}, u32[]{:S(2)}) collective-permute-start(f32[14,12288]{1,0:T(8,128)} %bitcast.152), channel_id=1, source_target_pairs={{0,256},{256,0},{1,257},{257,1},{2,258},{258,2},{3,259},{259,3},{4... | collective-permute-start | bytes 2064392 | tf_op jit(solution)/shard_map/ppermute | solution.py:20
  858.2 2.6 collective-permute-start.5
  859.5 4.8 collective-permute-start.6
  864.5 10.7 %collective-permute-start.7 = (f32[7,2,68,2]{3,2,1,0:T(8,128)S(1)}, f32[7,2,68,2]{3,2,1,0:T(8,128)S(1)}, u32[]{:S(2)}, u32[]{:S(2)}) collective-permute-start(f32[7,2,68,2]{3,2,1,0:T(8,128)S(1)} %get-tuple-element.131), channel_id=1, source_target_pairs={{0,1},{1,2},{2,3},{3,4},{4,5},{5,6},{6,7},{7,8},{8,9},{9,10},{10,1... | collective-permute-start | bytes 22856 | tf_op jit(solution)/shard_map/ppermute | solution.py:30
  869.2 10.7 %collective-permute-start.8 = (f32[7,2,68,2]{3,2,1,0:T(8,128)S(1)}, f32[7,2,68,2]{3,2,1,0:T(8,128)S(1)}, u32[]{:S(2)}, u32[]{:S(2)}) collective-permute-start(f32[7,2,68,2]{3,2,1,0:T(8,128)S(1)} %get-tuple-element.132), channel_id=1, source_target_pairs={{1,0},{2,1},{3,2},{4,3},{5,4},{6,5},{7,6},{8,7},{9,8},{10,9},{11,1... | collective-permute-start | bytes 22856 | tf_op jit(solution)/shard_map/ppermute | solution.py:31
  (8 other events, 5.1 us)
where the time goes:
time: 929 us; the launch traced here: 928 us
  blocking collectives  725 us (78%)
  local copies, waits for them, and re-layouts  142 us (15%)
  waiting for transfers between devices  23.6 us (3%)
  starting transfers between devices  21 us (2%)
  other arithmetic  16.2 us (2%)
    all_gather x2, blocking collectives, receive(): whole = lax.all_gather(given, ('lat', 'lon'), axis=1, tiled=True)  725 us
    scatter x2, local copies, waits for them, and re-layouts, extended(): ext.at[:, :, 2:2 + rows, cols + 2:cols + 4]  23.1 us
    scatter x2, local copies, waits for them, and re-layouts, extended(): ext.at[:, :, 2:2 + rows, 0:2]  18.7 us
  transfers between devices with their start and end apart: 10, of which 8 were waited for; matrix products, arithmetic and copies ran while one was open for 1% of the time, Pallas kernels for 0%

commit v1 on v0

v1 whole, which is shorter than its diff:
```python
import functools

import jax
import jax.numpy as jnp
from jax import lax
from jax.experimental import pallas as pl
from jax.experimental.pallas import tpu as pltpu
from jax.sharding import PartitionSpec as P

MESH = pl.DeviceIdType.MESH
DIFFUSION = 0.05
BUOYANCY = 0.5
STEP = 0.25
PAD = 8
UP, DOWN, LEFT, RIGHT = range(4)


def lane_take(value, index):
    return jnp.take_along_axis(value, index, axis=1, mode="promise_in_bounds")


def kernel(
    n_lat, n_lon, state, slots, cell, frac, turn, out,
    ext, whole_i, whole_f, pack, pack_from, don, gathered, idx, parts, top, bottom, left, right, flip,
    load_sem, send_a, recv_a, send_h, recv_h, send_i, recv_i, send_b, recv_b,
):
    comps, levels, rows, cols = state.shape[1:]
    n_slots = cell.shape[3]
    half = cols // 2
    side = 2 * rows
    q = lax.axis_index("panel")
    a = lax.axis_index("lat")
    b = lax.axis_index("lon")
    other = 1 - q
    first_a, last_a = a == 0, a == n_lat - 1
    first_b, last_b = b == 0, b == n_lon - 1

    neighbours = (
        (a > 0, (q, a - 1, b)),
        (a < n_lat - 1, (q, a + 1, b)),
        (b > 0, (q, a, b - 1)),
        (b < n_lon - 1, (q, a, b + 1)),
    )
    receivers = (
        (q, 0, b),
        (q, n_lat - 1, b),
        (q, b, 0),
        (q, b, n_lon - 1),
    )
    is_receiver = (first_a, last_a, first_b, last_b)
    own = (
        first_a,
        last_a,
        jnp.logical_and(first_a, first_b),
        jnp.logical_and(last_a, last_b),
    )

    def selector(role, k):
        return (q, k, b) if role < 2 else (q, k, a)

    def is_me(role, k):
        return (k == a) if role < 2 else jnp.logical_and(k == a, b == a)

    load = pltpu.make_async_copy(
        state.at[0], ext.at[0, :, :, pl.ds(PAD, rows), :], load_sem
    )
    load.start()

    barrier = pltpu.get_barrier_semaphore()

    def greet(device):
        pl.semaphore_signal(barrier, inc=1, device_id=device, device_id_type=MESH)

    @pl.loop(0, n_lon)
    def _(k):
        greet((other, a, k))

    for there, device in neighbours:
        pl.when(there)(functools.partial(greet, device))
    for role in range(4):
        pl.when(jnp.logical_not(own[role]))(functools.partial(greet, receivers[role]))

        @pl.when(is_receiver[role])
        def _():
            @pl.loop(0, n_lat)
            def _(k):
                pl.when(jnp.logical_not(is_me(role, k)))(
                    lambda: greet(selector(role, k))
                )

    whole_i[...] = jnp.zeros_like(whole_i)
    whole_f[...] = jnp.zeros_like(whole_f)
    for start in (0, half):
        whole_i[0:1, start : start + n_slots] = cell[0, 0]
        whole_f[0:1, start : start + n_slots] = turn[0, 0]
        whole_f[1:3, start : start + n_slots] = frac[0, 0, 0]
    cells = whole_i[0:1, :]
    turns = whole_f[0:1, :]
    cosine = jnp.cos(turns)
    sine = jnp.sin(turns)
    frac_t = whole_f[1:2, :]
    frac_p = whole_f[2:3, :]
    row = (cells * 33027) >> 22
    col = cells - row * (cols - 1)
    row_at = lax.broadcasted_iota(jnp.int32, (rows, cols), 0)
    row_full = jnp.broadcast_to(row, (rows, cols))
    weight_t = jnp.where(
        row_at == row_full,
        jnp.broadcast_to(1.0 - frac_t, (rows, cols)),
        jnp.where(row_at == row_full + 1, jnp.broadcast_to(frac_t, (rows, cols)), 0.0),
    )
    lane = lax.broadcasted_iota(jnp.int32, (rows, cols), 1)
    low_lane = lane < half
    lower_at = jnp.broadcast_to(col, (rows, cols))
    upper_at = lower_at + 1
    left_p = jnp.broadcast_to(1.0 - frac_p, (rows, cols))
    right_p = jnp.broadcast_to(frac_p, (rows, cols))
    lane8 = lax.broadcasted_iota(jnp.int32, (8, cols), 1)

    def inner(s, c, level, shift=0):
        return ext[s, c, level, PAD + shift : PAD + shift + rows, :]

    def donate(s):
        given = []
        for c in range(comps):
            low, high = inner(s, c, 0), inner(s, c, 1)
            one = jnp.where(low_lane, lane_take(low, lower_at), lane_take(high, lower_at))
            two = jnp.where(low_lane, lane_take(low, upper_at), lane_take(high, upper_at))
            mixed = (left_p * one + right_p * two) * weight_t
            given.append(jnp.sum(mixed, axis=0, keepdims=True))
        for i in (1, 4):
            x, y = given[i], given[i + 1]
            given[i], given[i + 1] = cosine * x - sine * y, sine * x + cosine * y
        for c in range(comps):
            don[s, c : c + 1, :] = given[c]
        don[s, comps : comps + 1, :] = jnp.zeros((1, cols), jnp.float32)

    def pack_sides(s):
        packed = jnp.zeros((rows, cols), jnp.float32)
        for f in range(comps * levels):
            turned = pltpu.roll(inner(s, f // levels, f % levels), 4 * f + 2, 1)
            packed = jnp.where(lane >> 2 == f, turned, packed)
        pack[s] = packed

    def halo_copies(s):
        e = ext.at[s]
        pairs = (
            (e.at[:, :, pl.ds(PAD, 8), :], e.at[:, :, pl.ds(PAD + rows, 8), :]),
            (e.at[:, :, pl.ds(PAD + rows - 8, 8), :], e.at[:, :, pl.ds(PAD - 8, 8), :]),
            (pack.at[s], pack_from.at[s, 1]),
            (pack.at[s], pack_from.at[s, 0]),
        )
        copies = []
        for to, (src, dst) in enumerate(pairs):
            copies.append(
                pltpu.make_async_remote_copy(
                    src_ref=src,
                    dst_ref=dst,
                    send_sem=send_h.at[s, to],
                    recv_sem=recv_h.at[s, to],
                    device_id=neighbours[to][1],
                    device_id_type=MESH,
                )
            )
        return copies

    def wait_bytes(ref, sem):
        pltpu.make_async_copy(ref, ref, sem).wait()

    def start_halo(s):
        for (there, _), copy in zip(neighbours, halo_copies(s)):
            pl.when(there)(copy.start)

    def start_a(s):
        @pl.loop(0, n_lon)
        def _(k):
            pltpu.make_async_remote_copy(
                src_ref=don.at[s],
                dst_ref=gathered.at[s, b],
                send_sem=send_a.at[s],
                recv_sem=recv_a.at[s],
                device_id=(other, a, k),
                device_id_type=MESH,
            ).start()

    ranges = ((0, 2 * cols), (2 * cols, 2 * cols), (4 * cols, side), (4 * cols + side, side))

    def index_copy(role, k):
        start, size = ranges[role]
        return pltpu.make_async_remote_copy(
            src_ref=slots.at[0, 0, :, pl.ds(start, size)],
            dst_ref=idx.at[:, pl.ds(start, size)],
            send_sem=send_i.at[role, k],
            recv_sem=recv_i.at[role],
            device_id=selector(role, k),
            device_id_type=MESH,
        )

    def each_selector(role, action):
        @pl.when(is_receiver[role])
        def _():
            @pl.loop(0, n_lat)
            def _(k):
                @pl.when(jnp.logical_not(is_me(role, k)))
                def _():
                    action(index_copy(role, k))

    buffers = (top, bottom, left, right)
    pieces = ((0, 2), (2, 2), (4, 1), (5, 1))

    def part_copy(s, role):
        start, size = pieces[role]
        return pltpu.make_async_remote_copy(
            src_ref=parts.at[s, pl.ds(start, size)],
            dst_ref=buffers[role].at[s, a],
            send_sem=send_b.at[s, role],
            recv_sem=recv_b.at[s, role],
            device_id=receivers[role],
            device_id_type=MESH,
        )

    def select(s):
        for tile in range(6):
            wanted = idx[0:1, tile * cols : (tile + 1) * cols] - a * (n_lon * n_slots)
            known = jnp.logical_and(wanted >= 0, wanted < n_lon * n_slots)
            wanted = jnp.where(known, wanted, 0)
            giver = ((wanted >> 4) * 21846) >> 16
            place = jnp.broadcast_to(wanted - giver * n_slots, (8, cols))
            giver = jnp.broadcast_to(jnp.where(known, giver, -1), (8, cols))

            def body(k, totals):
                block = gathered[s, k]
                mine = giver == k
                return tuple(
                    jnp.where(mine, lane_take(block, place + level * half), total)
                    for level, total in enumerate(totals)
                )

            zero = jnp.zeros((8, cols), jnp.float32)
            for level, total in enumerate(lax.fori_loop(0, n_lon, body, (zero, zero))):
                parts[s, tile, level] = total

    def start_b(s):
        for role in range(4):
            start, size = pieces[role]
            pl.when(jnp.logical_not(own[role]))(part_copy(s, role).start)

            @pl.when(own[role])
            def _():
                buffers[role][s, a] = parts[s, start : start + size]

    def take_rim(s):
        for role, buffer in enumerate(buffers):

            @pl.when(is_receiver[role])
            def _():
                if role % 2 == 0:
                    others = buffer.at[s, pl.ds(1, n_lat - 1)]
                else:
                    others = buffer.at[s, pl.ds(0, n_lat - 1)]
                sem = recv_b.at[s, role]
                if role < 2:
                    wait_bytes(others, sem)
                else:
                    pl.when(own[role])(lambda: wait_bytes(others, sem))
                    pl.when(jnp.logical_not(own[role]))(
                        lambda: wait_bytes(buffer.at[s], sem)
                    )
                total = jnp.sum(buffer[s], axis=0)
                if role < 2:
                    at = PAD - 2 if role == 0 else PAD + rows
                    for t in range(2):
                        for level in range(levels):
                            for c in range(comps):
                                ext[s, c, level, at + t : at + t + 1, :] = total[
                                    t, level, c : c + 1, :
                                ]
                else:
                    flip[...] = jnp.zeros_like(flip)
                    for level in range(levels):
                        both = (total[0, level], pltpu.roll(total[0, level], half, 1))
                        for t in range(2):
                            for c in range(comps):
                                at = 4 * (c * levels + level) + 2 * (role - 2) + t
                                flip[at : at + 1, :] = both[t][c : c + 1, :]
                    pack_from[s, role - 2] = flip[...].T[0:rows, :]

    def wait_halo(s):
        landed = (
            ext.at[s, :, :, pl.ds(PAD - 8, 8), :],
            ext.at[s, :, :, pl.ds(PAD + rows, 8), :],
            pack_from.at[s, 0],
            pack_from.at[s, 1],
        )
        for side_of, opposite in ((UP, DOWN), (DOWN, UP), (LEFT, RIGHT), (RIGHT, LEFT)):
            ref, sem = landed[side_of], recv_h.at[s, opposite]
            pl.when(neighbours[side_of][0])(functools.partial(wait_bytes, ref, sem))

    def rates(s, emit, chunk):
        for base in range(0, rows, chunk):
            lanes = lane[0:chunk]
            edge = jnp.where(
                lanes & 2 == 0,
                pack_from[s, 0, base : base + chunk, :],
                pack_from[s, 1, base : base + chunk, :],
            )

            def at(c, level, shift=0):
                low = PAD + base + shift
                return ext[s, c, level, low : low + chunk, :]

            for level in range(levels):
                u1, u2 = at(1, level) * (1.0 / 12.0), at(2, level) * (1.0 / 12.0)
                b1, b2 = at(4, level) * (1.0 / 12.0), at(5, level) * (1.0 / 12.0)

                def terms(c, with_b):
                    mid = at(c, level)
                    around = pltpu.roll(edge, (cols - 2 - 4 * (c * levels + level)) % cols, 1)
                    west1 = pltpu.roll(jnp.where(lanes == cols - 1, around, mid), 1, 1)
                    west2 = pltpu.roll(jnp.where(lanes >= cols - 2, around, mid), 2, 1)
                    east1 = pltpu.roll(jnp.where(lanes == 0, around, mid), cols - 1, 1)
                    east2 = pltpu.roll(jnp.where(lanes < 2, around, mid), cols - 2, 1)
                    north1, south1 = at(c, level, -1), at(c, level, 1)
                    d_lat = 8.0 * (south1 - north1) - (at(c, level, 2) - at(c, level, -2))
                    d_lon = 8.0 * (east1 - west1) - (east2 - west2)
                    lap = south1 + north1 + east1 + west1 + at(c, 1 - level) - 6.0 * mid
                    adv_u = u1 * d_lat + u2 * d_lon
                    adv_b = b1 * d_lat + b2 * d_lon if with_b else None
                    return mid, adv_u, adv_b, DIFFUSION * lap

                for c in range(3):
                    mid, adv_u, adv_b, lap = terms(c, True)
                    mid_b, adv_ub, adv_bb, lap_b = terms(c + 3, True)
                    moment = adv_bb - adv_u + lap
                    if c == 0:
                        moment = moment + BUOYANCY * at(6, level)
                    emit(c, level, base, mid, moment)
                    emit(c + 3, level, base, mid_b, adv_b - adv_ub + lap_b)
                mid, adv_u, _, lap = terms(6, False)
                emit(6, level, base, mid, lap - adv_u)

    chunk = 32

    def first_section(c, level, base, mid, rate):
        ext[1, c, level, PAD + base : PAD + base + chunk, :] = mid + STEP * rate

    def second_section(c, level, base, mid, rate):
        start = ext[0, c, level, PAD + base : PAD + base + chunk, :]
        out[0, c, level, base : base + chunk, :] = 0.5 * start + 0.5 * (mid + STEP * rate)

    load.wait()
    donate(0)
    pack_sides(0)

    count = n_lon
    for there, _ in neighbours:
        count = count + there.astype(jnp.int32)
    for role in range(4):
        count = count + jnp.logical_not(own[role]).astype(jnp.int32)
        count = count + jnp.where(
            is_receiver[role], n_lat - own[role].astype(jnp.int32), 0
        )
    pl.semaphore_wait(barrier, count)

    for s in range(2):
        if s == 1:
            donate(1)
            pack_sides(1)
        start_a(s)
        if s == 0:
            for role in range(4):
                each_selector(role, lambda copy: copy.start())
        start_halo(s)
        if s == 0:
            for role in range(4):
                start, size = ranges[role]
                here = idx.at[:, pl.ds(start, size)]

                @pl.when(own[role])
                def _():
                    idx[:, start : start + size] = slots[0, 0, :, start : start + size]

                pl.when(jnp.logical_not(own[role]))(
                    functools.partial(wait_bytes, here, recv_i.at[role])
                )
        wait_bytes(gathered.at[s], recv_a.at[s])
        select(s)
        start_b(s)
        wait_halo(s)
        take_rim(s)
        rates(s, first_section if s == 0 else second_section, chunk)

    for s in range(2):
        wait_bytes(gathered.at[s], send_a.at[s])
        for (there, _), copy in zip(neighbours, halo_copies(s)):
            pl.when(there)(copy.wait_send)
        for role in range(4):
            pl.when(jnp.logical_not(own[role]))(part_copy(s, role).wait_send)
    for role in range(4):
        each_selector(role, lambda copy: copy.wait_send())


def solution(mesh):
    n_lat, n_lon = mesh.shape["lat"], mesh.shape["lon"]

    def per_device(state, source_slot, donor_cell, donor_frac, donor_turn):
        _, comps, levels, rows, cols = state.shape
        f32, i32, dma = jnp.float32, jnp.int32, pltpu.SemaphoreType.DMA
        vmem = pl.BlockSpec(memory_space=pltpu.VMEM)
        return pl.pallas_call(
            functools.partial(kernel, n_lat, n_lon),
            out_shape=jax.ShapeDtypeStruct(state.shape, f32),
            in_specs=[pl.BlockSpec(memory_space=pl.ANY)] + [vmem] * 4,
            out_specs=vmem,
            scratch_shapes=[
                pltpu.VMEM((2, comps, levels, rows + 2 * PAD, cols), f32),
                pltpu.VMEM((8, cols), i32),
                pltpu.VMEM((8, cols), f32),
                pltpu.VMEM((2, rows, cols), f32),
                pltpu.VMEM((2, 2, rows, cols), f32),
                pltpu.VMEM((2, 8, cols), f32),
                pltpu.VMEM((2, n_lon, 8, cols), f32),
                pltpu.VMEM((1, 4 * cols + 4 * rows), i32),
                pltpu.VMEM((2, 6, levels, 8, cols), f32),
                pltpu.VMEM((2, n_lat, 2, levels, 8, cols), f32),
                pltpu.VMEM((2, n_lat, 2, levels, 8, cols), f32),
                pltpu.VMEM((2, n_lat, 1, levels, 8, cols), f32),
                pltpu.VMEM((2, n_lat, 1, levels, 8, cols), f32),
                pltpu.VMEM((cols, cols), f32),
                dma,
                dma((2,)),
                dma((2,)),
                dma((2, 4)),
                dma((2, 4)),
                dma((4, n_lat)),
                dma((4,)),
                dma((2, 4)),
                dma((2, 4)),
            ],
            compiler_params=pltpu.CompilerParams(
                collective_id=0, has_side_effects=True, vmem_limit_bytes=32 * 2**20
            ),
        )(state, source_slot, donor_cell, donor_frac, donor_turn)

    in_specs = (
        P("panel", None, None, "lat", "lon"),
        P("panel", "lat", "lon", None),
        P("panel", "lat", "lon", None),
        P("panel", "lat", "lon", None, None),
        P("panel", "lat", "lon", None),
    )
    out_specs = P("panel", None, None, "lat", "lon")
    return jax.shard_map(
        per_device, mesh=mesh, in_specs=in_specs, out_specs=out_specs, check_vma=False
    )
```

time: 929 us -> 75 us (0.08)
  blocking collectives: 725 us -> 0 us
  local copies, waits for them, and re-layouts: 142 us -> 4.46 us
  Pallas kernels: 0 us -> 70.3 us
  waiting for transfers between devices: 23.6 us -> 0 us
  starting transfers between devices: 21 us -> 0 us
  other arithmetic: 16.2 us -> 0 us
    all_gather x2 -> x0, blocking collectives: 725 us -> none  [receive(): whole = lax.all_gather(given, ('lat', 'lon'), axis=1, tiled=True)]
    pallas_call x0 -> x1, Pallas kernels: none -> 70.3 us  [per_device(): pl.pallas_call(functools.partial(kernel, n_lat, n_lon), out_shape=jax.Sha...]
    scatter x8 -> x0, local copies, waits for them, and re-layouts: 62.4 us -> none  [the longest x2 23.1 us: extended(): ext.at[:, :, 2:2 + rows, cols + 2:cols + 4]]
    gather x18 -> x0, local copies, waits for them, and re-layouts: 42.2 us -> none  [the longest x2 8.97 us: receive(): return jnp.take(partner, slots, axis=1)]
    ppermute x10 -> x0, waiting for transfers between devices: 23.6 us -> none  [the longest x4 11.8 us: with_halo(): after = lax.ppermute(initial, axis, down)]
    ppermute x10 -> x0, starting transfers between devices: 21 us -> none  [the longest x4 9.18 us: with_halo(): before = lax.ppermute(last, axis, up)]
    another operation x5 -> x0, local copies, waits for them, and re-layouts: 9.9 us -> none  [the longest x2 9.24 us: donate(): flat = field.reshape(comps, levels, rows * cols)]
  transfers between devices with their start and end apart: 10 -> 0, of which waited for: 8 -> 0; matrix products, arithmetic and copies ran while one was open for 1% -> 0% of each run, Pallas kernels for 0% -> 0%
where the time goes in v1:
time: 75 us; the launch traced here: 74.8 us
  Pallas kernels  70.3 us (94%)
  local copies, waits for them, and re-layouts  4.46 us (6%)
    pallas_call x1, Pallas kernels, per_device(): pl.pallas_call(functools.partial(kernel, n_lat, n_lon), out_shape=jax.Sha...  70.3 us
    unnamed x11, local copies, waits for them, and re-layouts  4.46 us

profile of v1, /device:TPU:1, one launch (start us, length us, event | category | flops | bytes accessed | tf_op | source)
XLA Modules:
  0.0 74.8 jit_solution(12889883083855794106)
XLA Ops:
  0.0 0.0 copy-start
  0.0 1.0 %copy-done = f32[1,7,2,64,128]{4,3,2,1,0:T(8,128)S(1)} copy-done((f32[1,7,2,64,128]{4,3,2,1,0:T(8,128)S(1)}, f32[1,7,2,64,128]{4,3,2,1,0:T(8,128)}, u32[]{:S(2)}) %copy-start) | copy-done | bytes 458776
  1.0 0.0 copy-start.1
  1.0 0.7 copy-done.1
  1.7 0.0 copy-start.2
  1.7 0.7 copy-done.2
  2.4 0.0 copy-start.3
  2.4 0.7 copy-done.3
  3.0 0.0 copy-start.4
  3.0 0.7 copy-done.4
  3.7 70.3 %shard_map.55 = f32[1,7,2,64,128]{4,3,2,1,0:T(8,128)S(1)} custom-call(f32[1,7,2,64,128]{4,3,2,1,0:T(8,128)S(1)} %copy-done, s32[1,1,1,768]{3,2,1,0:T(1,128)S(1)} %copy-done.1, s32[1,1,1,48]{3,2,1,0:T(1,128)S(1)} %copy-done.3, f32[1,1,1,2,48]{4,3,2,1,0:T(2,128)S(1)} %copy-done.2, f32[1,1,1,48]{3,2,1,0:T(1,128)S(1)} %copy-done.4), custom_call_target="tpu_custom_call" | custom-call | tf_op jit(solution)/shard_map/pallas_call | solution.py:410
  74.0 0.8 %copy.7 = f32[1,7,2,64,128]{4,3,2,1,0:T(8,128)} copy(f32[1,7,2,64,128]{4,3,2,1,0:T(8,128)S(1)} %shard_map.55) | data formatting | bytes 917504
Async XLA Ops:
  0.0 1.0 %copy-start = (f32[1,7,2,64,128]{4,3,2,1,0:T(8,128)S(1)}, f32[1,7,2,64,128]{4,3,2,1,0:T(8,128)}, u32[]{:S(2)}) copy-start(f32[1,7,2,64,128]{4,3,2,1,0:T(8,128)} %state.1) | copy-start | bytes 1376260
  1.0 0.7 copy-start.1
  1.7 0.7 copy-start.2
  2.4 0.7 copy-start.3
  3.0 0.7 copy-start.4

commit v2 on v1

v2 whole, which is shorter than its diff:
```python
import functools

import jax
import jax.numpy as jnp
from jax import lax
from jax.experimental import pallas as pl
from jax.experimental.pallas import tpu as pltpu
from jax.sharding import PartitionSpec as P

MESH = pl.DeviceIdType.MESH
DIFFUSION = 0.05
BUOYANCY = 0.5
STEP = 0.25
PAD = 8
UP, DOWN, LEFT, RIGHT = range(4)


def lane_take(value, index):
    return jnp.take_along_axis(value, index, axis=1, mode="promise_in_bounds")


def kernel(
    n_lat, n_lon, state, slots, cell, frac, turn, out,
    ext, cell_at, turn_at, frac_at, whole_i, whole_f, pack, pack_from, gathered, idx_rows, idx_sides,
    row_parts, side_parts, row_rim, side_rim, flip,
    load_sem, send_a, recv_a, send_h, recv_h, send_i, recv_i, send_b, recv_b,
):
    comps, levels, rows, cols = state.shape[1:]
    n_slots = cell.shape[3]
    half = cols // 2
    p = lax.axis_index("panel")
    a = lax.axis_index("lat")
    b = lax.axis_index("lon")
    other = 1 - p
    first_a, last_a = a == 0, a == n_lat - 1
    first_b, last_b = b == 0, b == n_lon - 1
    edge_a = jnp.logical_or(first_a, last_a)
    edge_b = jnp.logical_or(first_b, last_b)
    edge = jnp.logical_or(edge_a, edge_b)

    neighbours = (
        (a > 0, (p, a - 1, b)),
        (a < n_lat - 1, (p, a + 1, b)),
        (b > 0, (p, a, b - 1)),
        (b < n_lon - 1, (p, a, b + 1)),
    )

    loads = [
        pltpu.make_async_copy(cell.at[0, 0], cell_at, load_sem.at[1]),
        pltpu.make_async_copy(turn.at[0, 0], turn_at, load_sem.at[2]),
        pltpu.make_async_copy(frac.at[0, 0, 0], frac_at, load_sem.at[3]),
        pltpu.make_async_copy(
            state.at[0], ext.at[0, :, :, pl.ds(PAD, rows), :], load_sem.at[0]
        ),
    ]
    for load in loads:
        load.start()

    barrier = pltpu.get_barrier_semaphore()

    def greet(device):
        pl.semaphore_signal(barrier, inc=1, device_id=device, device_id_type=MESH)

    @pl.loop(0, n_lon)
    def _(k):
        greet((other, a, k))

    @pl.loop(1, n_lat)
    def _(k):
        greet((p, lax.rem(a + k, n_lat), b))

    for there, device in neighbours[2:]:
        pl.when(there)(functools.partial(greet, device))
    greeted = n_lon + n_lat - 1 + (b > 0).astype(jnp.int32) + (b < n_lon - 1).astype(jnp.int32)

    for load in loads[:3]:
        load.wait()
    whole_i[...] = jnp.zeros_like(whole_i)
    whole_f[...] = jnp.zeros_like(whole_f)
    for start in (0, half):
        whole_i[0:1, start : start + n_slots] = cell_at[...]
        whole_f[0:1, start : start + n_slots] = turn_at[...]
        whole_f[1:3, start : start + n_slots] = frac_at[...]
    cells = whole_i[0:1, :]
    turns = whole_f[0:1, :]
    cosine = jnp.cos(turns)
    sine = jnp.sin(turns)
    frac_t = whole_f[1:2, :]
    frac_p = whole_f[2:3, :]
    row = (cells * 33027) >> 22
    col = cells - row * (cols - 1)
    row_at = lax.broadcasted_iota(jnp.int32, (rows, cols), 0)
    row_full = jnp.broadcast_to(row, (rows, cols))
    weight_t = jnp.where(
        row_at == row_full,
        jnp.broadcast_to(1.0 - frac_t, (rows, cols)),
        jnp.where(row_at == row_full + 1, jnp.broadcast_to(frac_t, (rows, cols)), 0.0),
    )
    lane = lax.broadcasted_iota(jnp.int32, (rows, cols), 1)
    low_lane = lane < half
    lower_at = jnp.broadcast_to(col, (rows, cols))
    upper_at = lower_at + 1
    left_p = jnp.broadcast_to(1.0 - frac_p, (rows, cols))
    right_p = jnp.broadcast_to(frac_p, (rows, cols))
    lane8 = lax.broadcasted_iota(jnp.int32, (8, cols), 1)

    def inner(s, c, level, shift=0):
        return ext[s, c, level, PAD + shift : PAD + shift + rows, :]

    def donate(s):
        given = []
        for c in range(comps):
            low, high = inner(s, c, 0), inner(s, c, 1)
            one = jnp.where(low_lane, lane_take(low, lower_at), lane_take(high, lower_at))
            two = jnp.where(low_lane, lane_take(low, upper_at), lane_take(high, upper_at))
            mixed = (left_p * one + right_p * two) * weight_t
            given.append(jnp.sum(mixed, axis=0, keepdims=True))
        for i in (1, 4):
            x, y = given[i], given[i + 1]
            given[i], given[i + 1] = cosine * x - sine * y, sine * x + cosine * y
        for c in range(comps):
            gathered[s, a, c : c + 1, :] = given[c]
        gathered[s, a, comps : comps + 1, :] = jnp.zeros((1, cols), jnp.float32)

    def pack_sides(s):
        packed = jnp.zeros((rows, cols), jnp.float32)
        for f in range(comps * levels):
            turned = pltpu.roll(inner(s, f // levels, f % levels), 4 * f + 2, 1)
            packed = jnp.where(lane >> 2 == f, turned, packed)
        pack[s] = packed

    def halo_copies(s):
        e = ext.at[s]
        pairs = (
            (e.at[:, :, pl.ds(PAD, 8), :], e.at[:, :, pl.ds(PAD + rows, 8), :]),
            (e.at[:, :, pl.ds(PAD + rows - 8, 8), :], e.at[:, :, pl.ds(PAD - 8, 8), :]),
            (pack.at[s], pack_from.at[s, 1]),
            (pack.at[s], pack_from.at[s, 0]),
        )
        copies = []
        for to, (src, dst) in enumerate(pairs):
            copies.append(
                pltpu.make_async_remote_copy(
                    src_ref=src,
                    dst_ref=dst,
                    send_sem=send_h.at[s, to],
                    recv_sem=recv_h.at[s, to],
                    device_id=neighbours[to][1],
                    device_id_type=MESH,
                )
            )
        return copies

    def wait_bytes(ref, sem):
        pltpu.make_async_copy(ref, ref, sem).wait()

    def start_halo(s):
        for (there, _), copy in zip(neighbours, halo_copies(s)):
            pl.when(there)(copy.start)

    def start_a(s):
        @pl.loop(1, n_lat)
        def _(k):
            pltpu.make_async_remote_copy(
                src_ref=gathered.at[s, a],
                dst_ref=gathered.at[s, a],
                send_sem=send_a.at[s],
                recv_sem=recv_a.at[s],
                device_id=(p, lax.rem(a + k, n_lat), b),
                device_id_type=MESH,
            ).start()

    def wait_a(s, sem):
        wait_bytes(gathered.at[s, pl.ds(0, n_lat - 1)], sem.at[s])

    def send_slots():
        def send(start, dst, kind):
            size = dst.shape[-1]

            @pl.loop(0, n_lon)
            def _(k):
                pltpu.make_async_remote_copy(
                    src_ref=slots.at[0, 0, :, pl.ds(start, size)],
                    dst_ref=dst,
                    send_sem=send_i.at[kind],
                    recv_sem=recv_i.at[kind],
                    device_id=(other, a, k),
                    device_id_type=MESH,
                ).start()

        pl.when(first_a)(lambda: send(0, idx_rows.at[b], 0))
        pl.when(last_a)(lambda: send(2 * cols, idx_rows.at[b], 0))
        pl.when(first_b)(lambda: send(4 * cols, idx_sides.at[0], 1))
        pl.when(last_b)(lambda: send(4 * cols + 2 * rows, idx_sides.at[1], 1))

    def wait_slots():
        pl.when(edge_a)(lambda: wait_bytes(idx_rows, recv_i.at[0]))
        wait_bytes(idx_sides, recv_i.at[1])

    def pick(s, wanted):
        device = ((wanted >> 4) * 21846) >> 16
        place = jnp.broadcast_to(wanted - device * n_slots, (8, cols))
        row_of = device >> (n_lon.bit_length() - 1)
        giver = jnp.where(device - row_of * n_lon == b, row_of, -1)
        giver = jnp.broadcast_to(giver, (8, cols))
        totals = [jnp.zeros((8, cols), jnp.float32)] * levels
        places = [place + level * half for level in range(levels)]
        for k in range(n_lat):
            block = gathered[s, k]
            mine = giver == k
            for level in range(levels):
                totals[level] = jnp.where(mine, lane_take(block, places[level]), totals[level])
        return totals

    def send_parts(s):
        def to(src, dst, kind, k):
            return pltpu.make_async_remote_copy(
                src_ref=src,
                dst_ref=dst.at[s, b],
                send_sem=send_b.at[s, kind],
                recv_sem=recv_b.at[s, kind],
                device_id=(other, a, k),
                device_id_type=MESH,
            )

        for side in range(2):
            for level, total in enumerate(pick(s, idx_sides[side])):
                side_parts[s, side, level] = total
            to(side_parts.at[s, side], side_rim, 1, side * (n_lon - 1)).start()

        @pl.when(edge_a)
        def _():
            @pl.loop(0, n_lon)
            def _(k):
                for t in range(2):
                    for level, total in enumerate(
                        pick(s, idx_rows[k, :, t * cols : (t + 1) * cols])
                    ):
                        row_parts[s, k, t, level] = total
                to(row_parts.at[s, k], row_rim, 0, k).start()

    def take_rim(s):
        @pl.when(edge_a)
        def _():
            wait_bytes(row_rim.at[s], recv_b.at[s, 0])
            total = jnp.sum(row_rim[s], axis=0)

            def put(at):
                for t in range(2):
                    for level in range(levels):
                        for c in range(comps):
                            ext[s, c, level, at + t : at + t + 1, :] = total[t, level, c : c + 1, :]

            pl.when(first_a)(lambda: put(PAD - 2))
            pl.when(last_a)(lambda: put(PAD + rows))

        @pl.when(edge_b)
        def _():
            wait_bytes(side_rim.at[s], recv_b.at[s, 1])
            total = jnp.sum(side_rim[s], axis=0)

            def put(side):
                flip[...] = jnp.zeros_like(flip)
                for level in range(levels):
                    both = (total[level], pltpu.roll(total[level], half, 1))
                    for t in range(2):
                        for c in range(comps):
                            at = 4 * (c * levels + level) + 2 * side + t
                            flip[at : at + 1, :] = both[t][c : c + 1, :]
                pack_from[s, side] = flip[...].T[0:rows, :]

            pl.when(first_b)(lambda: put(0))
            pl.when(last_b)(lambda: put(1))

    def wait_halo(s):
        landed = (
            ext.at[s, :, :, pl.ds(PAD - 8, 8), :],
            ext.at[s, :, :, pl.ds(PAD + rows, 8), :],
            pack_from.at[s, 0],
            pack_from.at[s, 1],
        )
        for side_of, opposite in ((UP, DOWN), (DOWN, UP), (LEFT, RIGHT), (RIGHT, LEFT)):
            ref, sem = landed[side_of], recv_h.at[s, opposite]
            pl.when(neighbours[side_of][0])(functools.partial(wait_bytes, ref, sem))

    def rates(s, emit, chunk):
        for base in range(0, rows, chunk):
            lanes = lane[0:chunk]
            beside = jnp.where(
                lanes & 2 == 0,
                pack_from[s, 0, base : base + chunk, :],
                pack_from[s, 1, base : base + chunk, :],
            )

            def at(c, level, shift=0):
                low = PAD + base + shift
                return ext[s, c, level, low : low + chunk, :]

            for level in range(levels):
                u1, u2 = at(1, level) * (1.0 / 12.0), at(2, level) * (1.0 / 12.0)
                b1, b2 = at(4, level) * (1.0 / 12.0), at(5, level) * (1.0 / 12.0)

                def terms(c, with_b):
                    mid = at(c, level)
                    around = pltpu.roll(beside, (cols - 2 - 4 * (c * levels + level)) % cols, 1)
                    west1 = pltpu.roll(jnp.where(lanes == cols - 1, around, mid), 1, 1)
                    west2 = pltpu.roll(jnp.where(lanes >= cols - 2, around, mid), 2, 1)
                    east1 = pltpu.roll(jnp.where(lanes == 0, around, mid), cols - 1, 1)
                    east2 = pltpu.roll(jnp.where(lanes < 2, around, mid), cols - 2, 1)
                    north1, south1 = at(c, level, -1), at(c, level, 1)
                    d_lat = 8.0 * (south1 - north1) - (at(c, level, 2) - at(c, level, -2))
                    d_lon = 8.0 * (east1 - west1) - (east2 - west2)
                    lap = south1 + north1 + east1 + west1 + at(c, 1 - level) - 6.0 * mid
                    adv_u = u1 * d_lat + u2 * d_lon
                    adv_b = b1 * d_lat + b2 * d_lon if with_b else None
                    return mid, adv_u, adv_b, DIFFUSION * lap

                for c in range(3):
                    mid, adv_u, adv_b, lap = terms(c, True)
                    mid_b, adv_ub, adv_bb, lap_b = terms(c + 3, True)
                    moment = adv_bb - adv_u + lap
                    if c == 0:
                        moment = moment + BUOYANCY * at(6, level)
                    emit(c, level, base, mid, moment)
                    emit(c + 3, level, base, mid_b, adv_b - adv_ub + lap_b)
                mid, adv_u, _, lap = terms(6, False)
                emit(6, level, base, mid, lap - adv_u)

    chunk = rows

    def first_section(c, level, base, mid, rate):
        ext[1, c, level, PAD + base : PAD + base + chunk, :] = mid + STEP * rate

    def second_section(c, level, base, mid, rate):
        start = ext[0, c, level, PAD + base : PAD + base + chunk, :]
        out[0, c, level, base : base + chunk, :] = 0.5 * start + 0.5 * (mid + STEP * rate)

    def give(s):
        donate(s)
        if s == 0:
            pl.semaphore_wait(barrier, greeted)
        start_a(s)
        if s == 0:
            send_slots()
        pack_sides(s)
        start_halo(s)

    def first_half():
        rates(0, first_section, chunk)
        give(1)

    loads[3].wait()
    give(0)
    wait_halo(0)
    pl.when(jnp.logical_not(edge))(first_half)
    wait_a(0, recv_a)
    wait_slots()
    send_parts(0)

    @pl.when(edge)
    def _():
        take_rim(0)
        first_half()

    wait_a(1, recv_a)
    send_parts(1)
    wait_halo(1)
    pl.when(edge)(lambda: take_rim(1))
    rates(1, second_section, chunk)

    for s in range(2):
        wait_a(s, send_a)
        for (there, _), copy in zip(neighbours, halo_copies(s)):
            pl.when(there)(copy.wait_send)
        wait_bytes(side_parts.at[s], send_b.at[s, 1])
        pl.when(edge_a)(functools.partial(wait_bytes, row_parts.at[s], send_b.at[s, 0]))
    pl.when(edge_a)(lambda: wait_bytes(idx_rows, send_i.at[0]))
    pl.when(edge_b)(lambda: wait_bytes(idx_rows.at[pl.ds(0, n_lon // 2)], send_i.at[1]))


def solution(mesh):
    n_lat, n_lon = mesh.shape["lat"], mesh.shape["lon"]

    def per_device(state, source_slot, donor_cell, donor_frac, donor_turn):
        _, comps, levels, rows, cols = state.shape
        f32, i32, dma = jnp.float32, jnp.int32, pltpu.SemaphoreType.DMA
        vmem = pl.BlockSpec(memory_space=pltpu.VMEM)
        return pl.pallas_call(
            functools.partial(kernel, n_lat, n_lon),
            out_shape=jax.ShapeDtypeStruct(state.shape, f32),
            in_specs=[pl.BlockSpec(memory_space=pltpu.HBM)] * 5,
            out_specs=vmem,
            scratch_shapes=[
                pltpu.VMEM((2, comps, levels, rows + 2 * PAD, cols), f32),
                pltpu.VMEM((1, donor_cell.shape[3]), i32),
                pltpu.VMEM((1, donor_cell.shape[3]), f32),
                pltpu.VMEM((2, donor_cell.shape[3]), f32),
                pltpu.VMEM((8, cols), i32),
                pltpu.VMEM((8, cols), f32),
                pltpu.VMEM((2, rows, cols), f32),
                pltpu.VMEM((2, 2, rows, cols), f32),
                pltpu.VMEM((2, n_lat, 8, cols), f32),
                pltpu.VMEM((n_lon, 1, 2 * cols), i32),
                pltpu.VMEM((2, 1, 2 * rows), i32),
                pltpu.VMEM((2, n_lon, 2, levels, 8, cols), f32),
                pltpu.VMEM((2, 2, levels, 8, cols), f32),
                pltpu.VMEM((2, n_lon, 2, levels, 8, cols), f32),
                pltpu.VMEM((2, n_lon, levels, 8, cols), f32),
                pltpu.VMEM((cols, cols), f32),
                dma((4,)),
                dma((2,)),
                dma((2,)),
                dma((2, 4)),
                dma((2, 4)),
                dma((2,)),
                dma((2,)),
                dma((2, 2)),
                dma((2, 2)),
            ],
            compiler_params=pltpu.CompilerParams(
                collective_id=0, has_side_effects=True, vmem_limit_bytes=62 * 2**20
            ),
        )(state, source_slot, donor_cell, donor_frac, donor_turn)

    in_specs = (
        P("panel", None, None, "lat", "lon"),
        P("panel", "lat", "lon", None),
        P("panel", "lat", "lon", None),
        P("panel", "lat", "lon", None, None),
        P("panel", "lat", "lon", None),
    )
    out_specs = P("panel", None, None, "lat", "lon")
    return jax.shard_map(
        per_device, mesh=mesh, in_specs=in_specs, out_specs=out_specs, check_vma=False
    )
```

time: 75 us -> 50.5 us (0.67)
  the two profiles are of different devices: /device:TPU:1 before, /device:TPU:31 now
where the time goes in v2:
time: 50.5 us; the launch traced here: 50.3 us
  Pallas kernels  48.5 us (96%)
  local copies, waits for them, and re-layouts  1.82 us (4%)
    pallas_call x1, Pallas kernels, per_device(): pl.pallas_call(functools.partial(kernel, n_lat, n_lon), out_shape=jax.Sha...  48.5 us
    unnamed x1, local copies, waits for them, and re-layouts  1.82 us

profile of v2, /device:TPU:31, one launch (start us, length us, event | category | flops | bytes accessed | tf_op | source)
XLA Modules:
  0.0 50.3 jit_solution(17319938481785588098)
XLA Ops:
  0.0 48.5 %shard_map.55 = f32[1,7,2,64,128]{4,3,2,1,0:T(8,128)} custom-call(f32[1,7,2,64,128]{4,3,2,1,0:T(8,128)} %state.1, s32[1,1,1,768]{3,2,1,0:T(1,128)} %slots.1, s32[1,1,1,48]{3,2,1,0:T(1,128)} %cell.1, f32[1,1,1,2,48]{4,3,2,1,0:T(2,128)} %frac.1, f32[1,1,1,48]{3,2,1,0:T(1,128)} %turn.1), custom_call_target="tpu_custom_call" | custom-call | tf_op jit(solution)/shard_map/pallas_call | solution.py:388
  48.5 1.8 %copy.7 = f32[1,7,2,64,128]{4,3,2,1,0:T(8,128)} copy(f32[1,7,2,64,128]{4,3,2,1,0:T(8,128)} %shard_map.55) | data formatting | bytes 917504

commit v3 on v2

--- a/solution.py
+++ b/solution.py
@@ -15,13 +15,25 @@
 UP, DOWN, LEFT, RIGHT = range(4)
 
 
+def row_order(n_lon):
+    ways = sorted(range(n_lon), key=lambda d: -(2 if d & 6 == 4 else 1 if d & 6 else 0))
+    return [ways[i : i + 4] for i in range(0, n_lon, 4)]
+
+
+def pick_at(index, values):
+    result = values[-1]
+    for i, value in enumerate(values[:-1]):
+        result = jnp.where(index == i, value, result)
+    return result
+
+
 def lane_take(value, index):
     return jnp.take_along_axis(value, index, axis=1, mode="promise_in_bounds")
 
 
 def kernel(
     n_lat, n_lon, state, slots, cell, frac, turn, out,
-    ext, cell_at, turn_at, frac_at, whole_i, whole_f, pack, pack_from, gathered, idx_rows, idx_sides,
+    ext, cell_at, turn_at, frac_at, whole_i, whole_f, rows_to, rows_from, pack, pack_from, gathered, idx_rows, idx_sides,
     row_parts, side_parts, row_rim, side_rim, flip,
     load_sem, send_a, recv_a, send_h, recv_h, send_i, recv_i, send_b, recv_b,
 ):
@@ -102,7 +114,6 @@
     upper_at = lower_at + 1
     left_p = jnp.broadcast_to(1.0 - frac_p, (rows, cols))
     right_p = jnp.broadcast_to(frac_p, (rows, cols))
-    lane8 = lax.broadcasted_iota(jnp.int32, (8, cols), 1)
 
     def inner(s, c, level, shift=0):
         return ext[s, c, level, PAD + shift : PAD + shift + rows, :]
@@ -129,11 +140,16 @@
             packed = jnp.where(lane >> 2 == f, turned, packed)
         pack[s] = packed
 
+    def pack_rows(s):
+        for f in range(comps * levels):
+            c, level = f // levels, f % levels
+            rows_to[s, 0, f] = ext[s, c, level, PAD : PAD + 2, :]
+            rows_to[s, 1, f] = ext[s, c, level, PAD + rows - 2 : PAD + rows, :]
+
     def halo_copies(s):
-        e = ext.at[s]
         pairs = (
-            (e.at[:, :, pl.ds(PAD, 8), :], e.at[:, :, pl.ds(PAD + rows, 8), :]),
-            (e.at[:, :, pl.ds(PAD + rows - 8, 8), :], e.at[:, :, pl.ds(PAD - 8, 8), :]),
+            (rows_to.at[s, 0], rows_from.at[s, 1]),
+            (rows_to.at[s, 1], rows_from.at[s, 0]),
             (pack.at[s], pack_from.at[s, 1]),
             (pack.at[s], pack_from.at[s, 0]),
         )
@@ -159,14 +175,16 @@
             pl.when(there)(copy.start)
 
     def start_a(s):
-        @pl.loop(1, n_lat)
+        @pl.loop(0, n_lat - 1)
         def _(k):
+            step = (k + 1) >> 1
+            away = n_lat // 2 + jnp.where(k & 1 == 1, step, -step)
             pltpu.make_async_remote_copy(
                 src_ref=gathered.at[s, a],
                 dst_ref=gathered.at[s, a],
                 send_sem=send_a.at[s],
                 recv_sem=recv_a.at[s],
-                device_id=(p, lax.rem(a + k, n_lat), b),
+                device_id=(p, lax.rem(a + away, n_lat), b),
                 device_id_type=MESH,
             ).start()
 
@@ -230,14 +248,19 @@
 
         @pl.when(edge_a)
         def _():
-            @pl.loop(0, n_lon)
-            def _(k):
-                for t in range(2):
-                    for level, total in enumerate(
-                        pick(s, idx_rows[k, :, t * cols : (t + 1) * cols])
-                    ):
-                        row_parts[s, k, t, level] = total
-                to(row_parts.at[s, k], row_rim, 0, k).start()
+            order = row_order(n_lon)
+
+            @pl.loop(0, len(order))
+            def _(group):
+                to_whom = [b ^ pick_at(group, way) for way in zip(*order)]
+                for k in to_whom:
+                    for t in range(2):
+                        for level, total in enumerate(
+                            pick(s, idx_rows[k, :, t * cols : (t + 1) * cols])
+                        ):
+                            row_parts[s, k, t, level] = total
+                for k in to_whom:
+                    to(row_parts.at[s, k], row_rim, 0, k).start()
 
     def take_rim(s):
         @pl.when(edge_a)
@@ -273,18 +296,20 @@
             pl.when(last_b)(lambda: put(1))
 
     def wait_halo(s):
-        landed = (
-            ext.at[s, :, :, pl.ds(PAD - 8, 8), :],
-            ext.at[s, :, :, pl.ds(PAD + rows, 8), :],
-            pack_from.at[s, 0],
-            pack_from.at[s, 1],
-        )
+        landed = (rows_from.at[s, 0], rows_from.at[s, 1], pack_from.at[s, 0], pack_from.at[s, 1])
         for side_of, opposite in ((UP, DOWN), (DOWN, UP), (LEFT, RIGHT), (RIGHT, LEFT)):
-            ref, sem = landed[side_of], recv_h.at[s, opposite]
-            pl.when(neighbours[side_of][0])(functools.partial(wait_bytes, ref, sem))
-
-    def rates(s, emit, chunk):
-        for base in range(0, rows, chunk):
+
+            @pl.when(neighbours[side_of][0])
+            def _():
+                wait_bytes(landed[side_of], recv_h.at[s, opposite])
+                if side_of in (UP, DOWN):
+                    at = PAD - 2 if side_of == UP else PAD + rows
+                    for f in range(comps * levels):
+                        ext[s, f // levels, f % levels, at : at + 2, :] = rows_from[s, side_of, f]
+
+    def rates(s, emit, low_row=0, count=0):
+        chunk = count or rows
+        for base in (low_row,):
             lanes = lane[0:chunk]
             beside = jnp.where(
                 lanes & 2 == 0,
@@ -326,14 +351,12 @@
                 mid, adv_u, _, lap = terms(6, False)
                 emit(6, level, base, mid, lap - adv_u)
 
-    chunk = rows
-
     def first_section(c, level, base, mid, rate):
-        ext[1, c, level, PAD + base : PAD + base + chunk, :] = mid + STEP * rate
+        ext[1, c, level, PAD + base : PAD + base + mid.shape[0], :] = mid + STEP * rate
 
     def second_section(c, level, base, mid, rate):
-        start = ext[0, c, level, PAD + base : PAD + base + chunk, :]
-        out[0, c, level, base : base + chunk, :] = 0.5 * start + 0.5 * (mid + STEP * rate)
+        start = ext[0, c, level, PAD + base : PAD + base + mid.shape[0], :]
+        out[0, c, level, base : base + mid.shape[0], :] = 0.5 * start + 0.5 * (mid + STEP * rate)
 
     def give(s):
         donate(s)
@@ -343,30 +366,35 @@
         if s == 0:
             send_slots()
         pack_sides(s)
+        pack_rows(s)
         start_halo(s)
 
-    def first_half():
-        rates(0, first_section, chunk)
-        give(1)
+    def mend(s, emit):
+        take_rim(s)
+        inside = jnp.logical_not(edge_b)
+        pl.when(jnp.logical_and(first_a, inside))(lambda: rates(s, emit, 0, 8))
+        pl.when(jnp.logical_and(last_a, inside))(lambda: rates(s, emit, rows - 8, 8))
+        pl.when(edge_b)(lambda: rates(s, emit))
 
     loads[3].wait()
     give(0)
     wait_halo(0)
-    pl.when(jnp.logical_not(edge))(first_half)
+    rates(0, first_section)
+    pl.when(jnp.logical_not(edge))(lambda: give(1))
     wait_a(0, recv_a)
     wait_slots()
     send_parts(0)
 
     @pl.when(edge)
     def _():
-        take_rim(0)
-        first_half()
-
+        mend(0, first_section)
+        give(1)
+
+    wait_halo(1)
+    rates(1, second_section)
     wait_a(1, recv_a)
     send_parts(1)
-    wait_halo(1)
-    pl.when(edge)(lambda: take_rim(1))
-    rates(1, second_section, chunk)
+    pl.when(edge)(lambda: mend(1, second_section))
 
     for s in range(2):
         wait_a(s, send_a)
@@ -397,6 +425,8 @@
                 pltpu.VMEM((2, donor_cell.shape[3]), f32),
                 pltpu.VMEM((8, cols), i32),
                 pltpu.VMEM((8, cols), f32),
+                pltpu.VMEM((2, 2, comps * levels, 2, cols), f32),
+                pltpu.VMEM((2, 2, comps * levels, 2, cols), f32),
                 pltpu.VMEM((2, rows, cols), f32),
                 pltpu.VMEM((2, 2, rows, cols), f32),
                 pltpu.VMEM((2, n_lat, 8, cols), f32),
@@ -418,9 +448,14 @@
                 dma((2, 2)),
             ],
             compiler_params=pltpu.CompilerParams(
-                collective_id=0, has_side_effects=True, vmem_limit_bytes=62 * 2**20
+                collective_id=0, has_side_effects=True, vmem_limit_bytes=32 * 2**20
             ),
-        )(state, source_slot, donor_cell, donor_frac, donor_turn)
+        )(
+            *(
+                pltpu.with_memory_space_constraint(x, pltpu.HBM)
+                for x in (state, source_slot, donor_cell, donor_frac, donor_turn)
+            )
+        )
 
     in_specs = (
         P("panel", None, None, "lat", "lon"),

time: 50.5 us -> 46.1 us (0.913)
  the two profiles are of different devices: /device:TPU:31 before, /device:TPU:1 now
where the time goes in v3:
time: 46.1 us; the launch traced here: 45.4 us
  Pallas kernels  44.6 us (97%)
  local copies, waits for them, and re-layouts  0.77 us (2%)
    pallas_call x1, Pallas kernels, per_device(): pl.pallas_call(functools.partial(kernel, n_lat, n_lon), out_shape=jax.Sha...  44.6 us

profile of v3, /device:TPU:1, one launch (start us, length us, event | category | flops | bytes accessed | tf_op | source)
XLA Modules:
  0.0 45.4 jit_solution(3101982322129133075)
XLA Ops:
  0.0 44.6 %shard_map.55 = f32[1,7,2,64,128]{4,3,2,1,0:T(8,128)S(1)} custom-call(f32[1,7,2,64,128]{4,3,2,1,0:T(8,128)} %state.1, s32[1,1,1,768]{3,2,1,0:T(1,128)} %slots.1, s32[1,1,1,48]{3,2,1,0:T(1,128)} %cell.1, f32[1,1,1,2,48]{4,3,2,1,0:T(2,128)} %frac.1, f32[1,1,1,48]{3,2,1,0:T(1,128)} %turn.1), custom_call_target="tpu_custom_call" | custom-call | tf_op jit(solution)/shard_map/pallas_call | solution.py:416
  44.6 0.8 %copy.7 = f32[1,7,2,64,128]{4,3,2,1,0:T(8,128)} copy(f32[1,7,2,64,128]{4,3,2,1,0:T(8,128)S(1)} %shard_map.55) | data formatting | bytes 917504

commit v4 on v3

--- a/solution.py
+++ b/solution.py
@@ -33,7 +33,7 @@
 
 def kernel(
     n_lat, n_lon, state, slots, cell, frac, turn, out,
-    ext, cell_at, turn_at, frac_at, whole_i, whole_f, rows_to, rows_from, pack, pack_from, gathered, idx_rows, idx_sides,
+    ext, cell_at, turn_at, frac_at, whole_i, whole_f, rows_to, rows_from, pack, pack_from, gathered, dense, idx_rows, idx_sides,
     row_parts, side_parts, row_rim, side_rim, flip,
     load_sem, send_a, recv_a, send_h, recv_h, send_i, recv_i, send_b, recv_b,
 ):
@@ -110,10 +110,12 @@
     )
     lane = lax.broadcasted_iota(jnp.int32, (rows, cols), 1)
     low_lane = lane < half
-    lower_at = jnp.broadcast_to(col, (rows, cols))
-    upper_at = lower_at + 1
-    left_p = jnp.broadcast_to(1.0 - frac_p, (rows, cols))
-    right_p = jnp.broadcast_to(frac_p, (rows, cols))
+    col_at = jnp.broadcast_to(col, (rows, cols)) + jnp.where(low_lane, 0, 1)
+    weight = weight_t * jnp.where(
+        low_lane,
+        jnp.broadcast_to(1.0 - frac_p, (rows, cols)),
+        jnp.broadcast_to(frac_p, (rows, cols)),
+    )
 
     def inner(s, c, level, shift=0):
         return ext[s, c, level, PAD + shift : PAD + shift + rows, :]
@@ -121,11 +123,11 @@
     def donate(s):
         given = []
         for c in range(comps):
-            low, high = inner(s, c, 0), inner(s, c, 1)
-            one = jnp.where(low_lane, lane_take(low, lower_at), lane_take(high, lower_at))
-            two = jnp.where(low_lane, lane_take(low, upper_at), lane_take(high, upper_at))
-            mixed = (left_p * one + right_p * two) * weight_t
-            given.append(jnp.sum(mixed, axis=0, keepdims=True))
+            sums = []
+            for level in range(levels):
+                halves = jnp.sum(lane_take(inner(s, c, level), col_at) * weight, axis=0, keepdims=True)
+                sums.append(halves + pltpu.roll(halves, half, 1))
+            given.append(jnp.where(low_lane[0:1], sums[0], sums[1]))
         for i in (1, 4):
             x, y = given[i], given[i + 1]
             given[i], given[i + 1] = cosine * x - sine * y, sine * x + cosine * y
@@ -215,19 +217,33 @@
         pl.when(edge_a)(lambda: wait_bytes(idx_rows, recv_i.at[0]))
         wait_bytes(idx_sides, recv_i.at[1])
 
+    groups = -(-n_lat * n_slots // cols)
+    lane8 = lane[0:8]
+
+    def settle(s):
+        for level in range(levels):
+            totals = [jnp.zeros((8, cols), jnp.float32)] * groups
+            for k in range(n_lat):
+                low, high = k * n_slots, (k + 1) * n_slots
+                turned = pltpu.roll(gathered[s, k], (low - level * half) % cols, 1)
+                for g in range(low // cols, (high - 1) // cols + 1):
+                    here = jnp.logical_and(lane8 >= low - g * cols, lane8 < high - g * cols)
+                    totals[g] = jnp.where(here, turned, totals[g])
+            for g in range(groups):
+                dense[s, level, g] = totals[g]
+
     def pick(s, wanted):
         device = ((wanted >> 4) * 21846) >> 16
-        place = jnp.broadcast_to(wanted - device * n_slots, (8, cols))
         row_of = device >> (n_lon.bit_length() - 1)
-        giver = jnp.where(device - row_of * n_lon == b, row_of, -1)
-        giver = jnp.broadcast_to(giver, (8, cols))
+        number = wanted - (device - row_of) * n_slots
+        group = jnp.where(device - row_of * n_lon == b, number >> (cols.bit_length() - 1), -1)
+        group = jnp.broadcast_to(group, (8, cols))
+        place = jnp.broadcast_to(number & (cols - 1), (8, cols))
         totals = [jnp.zeros((8, cols), jnp.float32)] * levels
-        places = [place + level * half for level in range(levels)]
-        for k in range(n_lat):
-            block = gathered[s, k]
-            mine = giver == k
+        for g in range(groups):
+            mine = group == g
             for level in range(levels):
-                totals[level] = jnp.where(mine, lane_take(block, places[level]), totals[level])
+                totals[level] = jnp.where(mine, lane_take(dense[s, level, g], place), totals[level])
         return totals
 
     def send_parts(s):
@@ -241,6 +257,7 @@
                 device_id_type=MESH,
             )
 
+        settle(s)
         for side in range(2):
             for level, total in enumerate(pick(s, idx_sides[side])):
                 side_parts[s, side, level] = total
@@ -369,26 +386,64 @@
         pack_rows(s)
         start_halo(s)
 
+    def mend_side(s):
+        rim = jnp.where(first_b, pack_from[s, 0], pack_from[s, 1])
+        spot = lane & 3
+        near_w, far_w = pltpu.roll(rim, 1, 1), pltpu.roll(rim, 2, 1)
+        near_e, far_e = pltpu.roll(rim, cols - 1, 1), pltpu.roll(rim, cols - 2, 1)
+        slope = jnp.where(
+            spot == 2,
+            far_w - 8.0 * near_w,
+            jnp.where(spot == 3, far_w, jnp.where(spot == 1, 8.0 * near_e - far_e, -far_e)),
+        ) * (1.0 / 12.0)
+        lap = jnp.where(spot == 2, near_w, jnp.where(spot == 1, near_e, 0.0))
+        per_comp = 4 * levels
+        within = lane & (per_comp - 1)
+        u2 = lane_take(pack[s], within + 2 * per_comp)
+        b2 = lane_take(pack[s], within + 5 * per_comp)
+        swap = 3 * per_comp
+        partner = jnp.where(
+            lane < swap,
+            pltpu.roll(slope, cols - swap, 1),
+            jnp.where(lane < 2 * swap, pltpu.roll(slope, swap, 1), 0.0),
+        )
+        scale = STEP if s == 0 else 0.5 * STEP
+        change = scale * (DIFFUSION * lap - u2 * slope + b2 * partner)
+        outer = jnp.logical_or(lane >= cols - 2, lane < 2)
+        for f in range(comps * levels):
+            c, level = f // levels, f % levels
+            here = jnp.where(outer, pltpu.roll(change, (cols - 2 - 4 * f) % cols, 1), 0.0)
+            if s == 0:
+                ext[1, c, level, PAD : PAD + rows, :] = inner(1, c, level) + here
+            else:
+                out[0, c, level] = out[0, c, level] + here
+
     def mend(s, emit):
         take_rim(s)
-        inside = jnp.logical_not(edge_b)
-        pl.when(jnp.logical_and(first_a, inside))(lambda: rates(s, emit, 0, 8))
-        pl.when(jnp.logical_and(last_a, inside))(lambda: rates(s, emit, rows - 8, 8))
-        pl.when(edge_b)(lambda: rates(s, emit))
+        pl.when(edge_b)(lambda: mend_side(s))
+        pl.when(first_a)(lambda: rates(s, emit, 0, 8))
+        pl.when(last_a)(lambda: rates(s, emit, rows - 8, 8))
+
+    for s in range(2):
+
+        @pl.when(first_b)
+        def _():
+            pack_from[s, 0] = jnp.zeros((rows, cols), jnp.float32)
+
+        @pl.when(last_b)
+        def _():
+            pack_from[s, 1] = jnp.zeros((rows, cols), jnp.float32)
 
     loads[3].wait()
     give(0)
     wait_halo(0)
     rates(0, first_section)
-    pl.when(jnp.logical_not(edge))(lambda: give(1))
     wait_a(0, recv_a)
     wait_slots()
     send_parts(0)
 
-    @pl.when(edge)
-    def _():
-        mend(0, first_section)
-        give(1)
+    pl.when(edge)(lambda: mend(0, first_section))
+    give(1)
 
     wait_halo(1)
     rates(1, second_section)
@@ -430,6 +485,7 @@
                 pltpu.VMEM((2, rows, cols), f32),
                 pltpu.VMEM((2, 2, rows, cols), f32),
                 pltpu.VMEM((2, n_lat, 8, cols), f32),
+                pltpu.VMEM((2, levels, -(-n_lat * donor_cell.shape[3] // cols), 8, cols), f32),
                 pltpu.VMEM((n_lon, 1, 2 * cols), i32),
                 pltpu.VMEM((2, 1, 2 * rows), i32),
                 pltpu.VMEM((2, n_lon, 2, levels, 8, cols), f32),

time: 46.1 us -> 44.1 us (0.957); the launches traced: 45.4 us -> 44 us
  Pallas kernels: 44.6 us -> 43.2 us
    pallas_call x1, Pallas kernels: 44.6 us -> 43.2 us  [per_device(): pl.pallas_call(functools.partial(kernel, n_lat, n_lon), out_shape=jax.Sha...]
where the time goes in v4:
time: 44.1 us; the launch traced here: 44 us
  Pallas kernels  43.2 us (98%)
  local copies, waits for them, and re-layouts  0.77 us (2%)
    pallas_call x1, Pallas kernels, per_device(): pl.pallas_call(functools.partial(kernel, n_lat, n_lon), out_shape=jax.Sha...  43.2 us

profile of v4, /device:TPU:1, one launch (start us, length us, event | category | flops | bytes accessed | tf_op | source)
XLA Modules:
  0.0 44.0 jit_solution(17053774729960084303)
XLA Ops:
  0.0 43.2 %shard_map.55 = f32[1,7,2,64,128]{4,3,2,1,0:T(8,128)S(1)} custom-call(f32[1,7,2,64,128]{4,3,2,1,0:T(8,128)} %state.1, s32[1,1,1,768]{3,2,1,0:T(1,128)} %slots.1, s32[1,1,1,48]{3,2,1,0:T(1,128)} %cell.1, f32[1,1,1,2,48]{4,3,2,1,0:T(2,128)} %frac.1, f32[1,1,1,48]{3,2,1,0:T(1,128)} %turn.1), custom_call_target="tpu_custom_call" | custom-call | tf_op jit(solution)/shard_map/pallas_call | solution.py:471
  43.2 0.8 %copy.7 = f32[1,7,2,64,128]{4,3,2,1,0:T(8,128)} copy(f32[1,7,2,64,128]{4,3,2,1,0:T(8,128)S(1)} %shard_map.55) | data formatting | bytes 917504

commit v5 on v4

--- a/solution.py
+++ b/solution.py
@@ -68,18 +68,22 @@
     for load in loads:
         load.start()
 
+    def far_first(k):
+        step = (k + 1) >> 1
+        return n_lat // 2 + jnp.where(k & 1 == 1, step, -step)
+
     barrier = pltpu.get_barrier_semaphore()
 
     def greet(device):
         pl.semaphore_signal(barrier, inc=1, device_id=device, device_id_type=MESH)
+
+    @pl.loop(0, n_lat - 1)
+    def _(k):
+        greet((p, lax.rem(a + far_first(k), n_lat), b))
 
     @pl.loop(0, n_lon)
     def _(k):
         greet((other, a, k))
-
-    @pl.loop(1, n_lat)
-    def _(k):
-        greet((p, lax.rem(a + k, n_lat), b))
 
     for there, device in neighbours[2:]:
         pl.when(there)(functools.partial(greet, device))
@@ -133,7 +137,6 @@
             given[i], given[i + 1] = cosine * x - sine * y, sine * x + cosine * y
         for c in range(comps):
             gathered[s, a, c : c + 1, :] = given[c]
-        gathered[s, a, comps : comps + 1, :] = jnp.zeros((1, cols), jnp.float32)
 
     def pack_sides(s):
         packed = jnp.zeros((rows, cols), jnp.float32)
@@ -179,19 +182,17 @@
     def start_a(s):
         @pl.loop(0, n_lat - 1)
         def _(k):
-            step = (k + 1) >> 1
-            away = n_lat // 2 + jnp.where(k & 1 == 1, step, -step)
             pltpu.make_async_remote_copy(
-                src_ref=gathered.at[s, a],
-                dst_ref=gathered.at[s, a],
+                src_ref=gathered.at[s, a, pl.ds(0, comps)],
+                dst_ref=gathered.at[s, a, pl.ds(0, comps)],
                 send_sem=send_a.at[s],
                 recv_sem=recv_a.at[s],
-                device_id=(p, lax.rem(a + away, n_lat), b),
+                device_id=(p, lax.rem(a + far_first(k), n_lat), b),
                 device_id_type=MESH,
             ).start()
 
     def wait_a(s, sem):
-        wait_bytes(gathered.at[s, pl.ds(0, n_lat - 1)], sem.at[s])
+        wait_bytes(gathered.at[s, pl.ds(0, n_lat - 1), pl.ds(0, comps)], sem.at[s])
 
     def send_slots():
         def send(start, dst, kind):
@@ -250,7 +251,7 @@
         def to(src, dst, kind, k):
             return pltpu.make_async_remote_copy(
                 src_ref=src,
-                dst_ref=dst.at[s, b],
+                dst_ref=dst.at[s, b, :, :, pl.ds(0, comps)] if kind == 0 else dst.at[s, b, :, pl.ds(0, comps)],
                 send_sem=send_b.at[s, kind],
                 recv_sem=recv_b.at[s, kind],
                 device_id=(other, a, k),
@@ -261,7 +262,7 @@
         for side in range(2):
             for level, total in enumerate(pick(s, idx_sides[side])):
                 side_parts[s, side, level] = total
-            to(side_parts.at[s, side], side_rim, 1, side * (n_lon - 1)).start()
+            to(side_parts.at[s, side, :, pl.ds(0, comps)], side_rim, 1, side * (n_lon - 1)).start()
 
         @pl.when(edge_a)
         def _():
@@ -277,12 +278,12 @@
                         ):
                             row_parts[s, k, t, level] = total
                 for k in to_whom:
-                    to(row_parts.at[s, k], row_rim, 0, k).start()
+                    to(row_parts.at[s, k, :, :, pl.ds(0, comps)], row_rim, 0, k).start()
 
     def take_rim(s):
         @pl.when(edge_a)
         def _():
-            wait_bytes(row_rim.at[s], recv_b.at[s, 0])
+            wait_bytes(row_rim.at[s, :, :, :, pl.ds(0, comps)], recv_b.at[s, 0])
             total = jnp.sum(row_rim[s], axis=0)
 
             def put(at):
@@ -296,7 +297,7 @@
 
         @pl.when(edge_b)
         def _():
-            wait_bytes(side_rim.at[s], recv_b.at[s, 1])
+            wait_bytes(side_rim.at[s, :, :, pl.ds(0, comps)], recv_b.at[s, 1])
             total = jnp.sum(side_rim[s], axis=0)
 
             def put(side):
@@ -445,20 +446,24 @@
     pl.when(edge)(lambda: mend(0, first_section))
     give(1)
 
+    wait_a(1, recv_a)
+    send_parts(1)
     wait_halo(1)
     rates(1, second_section)
-    wait_a(1, recv_a)
-    send_parts(1)
-    pl.when(edge)(lambda: mend(1, second_section))
-
     for s in range(2):
         wait_a(s, send_a)
         for (there, _), copy in zip(neighbours, halo_copies(s)):
             pl.when(there)(copy.wait_send)
-        wait_bytes(side_parts.at[s], send_b.at[s, 1])
-        pl.when(edge_a)(functools.partial(wait_bytes, row_parts.at[s], send_b.at[s, 0]))
     pl.when(edge_a)(lambda: wait_bytes(idx_rows, send_i.at[0]))
     pl.when(edge_b)(lambda: wait_bytes(idx_rows.at[pl.ds(0, n_lon // 2)], send_i.at[1]))
+
+    pl.when(edge)(lambda: mend(1, second_section))
+
+    for s in range(2):
+        wait_bytes(side_parts.at[s, :, :, pl.ds(0, comps)], send_b.at[s, 1])
+        pl.when(edge_a)(
+            functools.partial(wait_bytes, row_parts.at[s, :, :, :, pl.ds(0, comps)], send_b.at[s, 0])
+        )
 
 
 def solution(mesh):

time: 44.1 us -> 42.7 us (0.968)
  Pallas kernels: 43.2 us -> 41.8 us
    pallas_call x1, Pallas kernels: 43.2 us -> 41.8 us  [per_device(): pl.pallas_call(functools.partial(kernel, n_lat, n_lon), out_shape=jax.Sha...]
where the time goes in v5:
time: 42.7 us; the launch traced here: 42.5 us
  Pallas kernels  41.8 us (98%)
  local copies, waits for them, and re-layouts  0.77 us (2%)
    pallas_call x1, Pallas kernels, per_device(): pl.pallas_call(functools.partial(kernel, n_lat, n_lon), out_shape=jax.Sha...  41.8 us

profile of v5, /device:TPU:1, one launch (start us, length us, event | category | flops | bytes accessed | tf_op | source)
XLA Modules:
  0.0 42.5 jit_solution(16998225901961361803)
XLA Ops:
  0.0 41.8 %shard_map.55 = f32[1,7,2,64,128]{4,3,2,1,0:T(8,128)S(1)} custom-call(f32[1,7,2,64,128]{4,3,2,1,0:T(8,128)} %state.1, s32[1,1,1,768]{3,2,1,0:T(1,128)} %slots.1, s32[1,1,1,48]{3,2,1,0:T(1,128)} %cell.1, f32[1,1,1,2,48]{4,3,2,1,0:T(2,128)} %frac.1, f32[1,1,1,48]{3,2,1,0:T(1,128)} %turn.1), custom_call_target="tpu_custom_call" | custom-call | tf_op jit(solution)/shard_map/pallas_call | solution.py:476
  41.8 0.8 %copy.7 = f32[1,7,2,64,128]{4,3,2,1,0:T(8,128)} copy(f32[1,7,2,64,128]{4,3,2,1,0:T(8,128)S(1)} %shard_map.55) | data formatting | bytes 917504

commit v6 on v5

--- a/solution.py
+++ b/solution.py
@@ -17,7 +17,8 @@
 
 def row_order(n_lon):
     ways = sorted(range(n_lon), key=lambda d: -(2 if d & 6 == 4 else 1 if d & 6 else 0))
-    return [ways[i : i + 4] for i in range(0, n_lon, 4)]
+    size = min(4, n_lon // 2)
+    return [ways[i : i + size] for i in range(0, n_lon, size)]
 
 
 def pick_at(index, values):
@@ -34,8 +35,8 @@
 def kernel(
     n_lat, n_lon, state, slots, cell, frac, turn, out,
     ext, cell_at, turn_at, frac_at, whole_i, whole_f, rows_to, rows_from, pack, pack_from, gathered, dense, idx_rows, idx_sides,
-    row_parts, side_parts, row_rim, side_rim, flip,
-    load_sem, send_a, recv_a, send_h, recv_h, send_i, recv_i, send_b, recv_b,
+    row_parts, side_parts, row_rim, side_rim, flip, helped, dense_x, row_parts_x,
+    load_sem, send_a, recv_a, send_h, recv_h, send_i, recv_i, send_b, recv_b, send_x, recv_x, send_y,
 ):
     comps, levels, rows, cols = state.shape[1:]
     n_slots = cell.shape[3]
@@ -49,6 +50,8 @@
     edge_a = jnp.logical_or(first_a, last_a)
     edge_b = jnp.logical_or(first_b, last_b)
     edge = jnp.logical_or(edge_a, edge_b)
+    twin = b ^ 1
+    helps = jnp.logical_and(edge_a, jnp.logical_or(twin == 0, twin == n_lon - 1))
 
     neighbours = (
         (a > 0, (p, a - 1, b)),
@@ -85,9 +88,16 @@
     def _(k):
         greet((other, a, k))
 
+    @pl.when(helps)
+    def _():
+        @pl.loop(0, n_lat)
+        def _(k):
+            greet((p, k, twin))
+
     for there, device in neighbours[2:]:
         pl.when(there)(functools.partial(greet, device))
     greeted = n_lon + n_lat - 1 + (b > 0).astype(jnp.int32) + (b < n_lon - 1).astype(jnp.int32)
+    greeted = greeted + jnp.where(edge_b, 2, 0)
 
     for load in loads[:3]:
         load.wait()
@@ -181,7 +191,8 @@
 
     def start_a(s):
         @pl.loop(0, n_lat - 1)
-        def _(k):
+        def _(i):
+            k = i if s == 0 else jnp.where(edge_a, n_lat - 2 - i, i)
             pltpu.make_async_remote_copy(
                 src_ref=gathered.at[s, a, pl.ds(0, comps)],
                 dst_ref=gathered.at[s, a, pl.ds(0, comps)],
@@ -190,6 +201,16 @@
                 device_id=(p, lax.rem(a + far_first(k), n_lat), b),
                 device_id_type=MESH,
             ).start()
+
+    def help_copy(i):
+        return pltpu.make_async_remote_copy(
+            src_ref=gathered.at[1, a, pl.ds(0, comps)],
+            dst_ref=helped.at[a, pl.ds(0, comps)],
+            send_sem=send_x.at[i],
+            recv_sem=recv_x,
+            device_id=(p, i * (n_lat - 1), twin),
+            device_id_type=MESH,
+        )
 
     def wait_a(s, sem):
         wait_bytes(gathered.at[s, pl.ds(0, n_lat - 1), pl.ds(0, comps)], sem.at[s])
@@ -221,64 +242,77 @@
     groups = -(-n_lat * n_slots // cols)
     lane8 = lane[0:8]
 
-    def settle(s):
+    def settle(block_of, packed):
         for level in range(levels):
             totals = [jnp.zeros((8, cols), jnp.float32)] * groups
             for k in range(n_lat):
                 low, high = k * n_slots, (k + 1) * n_slots
-                turned = pltpu.roll(gathered[s, k], (low - level * half) % cols, 1)
+                turned = pltpu.roll(block_of[k], (low - level * half) % cols, 1)
                 for g in range(low // cols, (high - 1) // cols + 1):
                     here = jnp.logical_and(lane8 >= low - g * cols, lane8 < high - g * cols)
                     totals[g] = jnp.where(here, turned, totals[g])
             for g in range(groups):
-                dense[s, level, g] = totals[g]
-
-    def pick(s, wanted):
+                packed[level, g] = totals[g]
+
+    def pick(packed, column, wanted):
         device = ((wanted >> 4) * 21846) >> 16
         row_of = device >> (n_lon.bit_length() - 1)
         number = wanted - (device - row_of) * n_slots
-        group = jnp.where(device - row_of * n_lon == b, number >> (cols.bit_length() - 1), -1)
+        group = jnp.where(device - row_of * n_lon == column, number >> (cols.bit_length() - 1), -1)
         group = jnp.broadcast_to(group, (8, cols))
         place = jnp.broadcast_to(number & (cols - 1), (8, cols))
         totals = [jnp.zeros((8, cols), jnp.float32)] * levels
         for g in range(groups):
             mine = group == g
             for level in range(levels):
-                totals[level] = jnp.where(mine, lane_take(dense[s, level, g], place), totals[level])
+                totals[level] = jnp.where(mine, lane_take(packed[level, g], place), totals[level])
         return totals
 
+    order = row_order(n_lon)
+    late = len(order) // 2
+
+    def part_copy(s, src, dst, sem, kind, k):
+        return pltpu.make_async_remote_copy(
+            src_ref=src,
+            dst_ref=dst,
+            send_sem=sem,
+            recv_sem=recv_b.at[s, kind],
+            device_id=(other, a, k),
+            device_id_type=MESH,
+        )
+
+    def send_rows(s, packed, column, held, sem, first, last):
+        @pl.loop(first, last)
+        def _(group):
+            to_whom = [column ^ pick_at(group, way) for way in zip(*order)]
+            for k in to_whom:
+                for t in range(2):
+                    wanted = idx_rows[k, :, t * cols : (t + 1) * cols]
+                    for level, total in enumerate(pick(packed, column, wanted)):
+                        held[k, t, level] = total
+            for k in to_whom:
+                src = held.at[k, :, :, pl.ds(0, comps)]
+                dst = row_rim.at[s, column, :, :, pl.ds(0, comps)]
+                part_copy(s, src, dst, sem, 0, k).start()
+
     def send_parts(s):
-        def to(src, dst, kind, k):
-            return pltpu.make_async_remote_copy(
-                src_ref=src,
-                dst_ref=dst.at[s, b, :, :, pl.ds(0, comps)] if kind == 0 else dst.at[s, b, :, pl.ds(0, comps)],
-                send_sem=send_b.at[s, kind],
-                recv_sem=recv_b.at[s, kind],
-                device_id=(other, a, k),
-                device_id_type=MESH,
-            )
-
-        settle(s)
+        settle(gathered.at[s], dense.at[s])
         for side in range(2):
-            for level, total in enumerate(pick(s, idx_sides[side])):
+            for level, total in enumerate(pick(dense.at[s], b, idx_sides[side])):
                 side_parts[s, side, level] = total
-            to(side_parts.at[s, side, :, pl.ds(0, comps)], side_rim, 1, side * (n_lon - 1)).start()
+            src = side_parts.at[s, side, :, pl.ds(0, comps)]
+            dst = side_rim.at[s, b, :, pl.ds(0, comps)]
+            part_copy(s, src, dst, send_b.at[s, 1], 1, side * (n_lon - 1)).start()
 
         @pl.when(edge_a)
         def _():
-            order = row_order(n_lon)
-
-            @pl.loop(0, len(order))
-            def _(group):
-                to_whom = [b ^ pick_at(group, way) for way in zip(*order)]
-                for k in to_whom:
-                    for t in range(2):
-                        for level, total in enumerate(
-                            pick(s, idx_rows[k, :, t * cols : (t + 1) * cols])
-                        ):
-                            row_parts[s, k, t, level] = total
-                for k in to_whom:
-                    to(row_parts.at[s, k, :, :, pl.ds(0, comps)], row_rim, 0, k).start()
+            last = len(order) if s == 0 else jnp.where(edge_b, late, len(order))
+            send_rows(s, dense.at[s], b, row_parts.at[s], send_b.at[s, 0], 0, last)
+
+    def help_out():
+        wait_bytes(helped.at[:, pl.ds(0, comps)], recv_x)
+        settle(helped, dense_x)
+        send_rows(1, dense_x, twin, row_parts_x, send_y, late, len(order))
 
     def take_rim(s):
         @pl.when(edge_a)
@@ -380,6 +414,9 @@
         donate(s)
         if s == 0:
             pl.semaphore_wait(barrier, greeted)
+        if s == 1:
+            for i in range(2):
+                pl.when(edge_b)(help_copy(i).start)
         start_a(s)
         if s == 0:
             send_slots()
@@ -450,6 +487,7 @@
     send_parts(1)
     wait_halo(1)
     rates(1, second_section)
+    pl.when(helps)(help_out)
     for s in range(2):
         wait_a(s, send_a)
         for (there, _), copy in zip(neighbours, halo_copies(s)):
@@ -461,9 +499,17 @@
 
     for s in range(2):
         wait_bytes(side_parts.at[s, :, :, pl.ds(0, comps)], send_b.at[s, 1])
-        pl.when(edge_a)(
-            functools.partial(wait_bytes, row_parts.at[s, :, :, :, pl.ds(0, comps)], send_b.at[s, 0])
-        )
+    shared = n_lon * late // len(order)
+    sent = [row_parts.at[s, :, :, :, pl.ds(0, comps)] for s in range(2)]
+    half_sent = row_parts.at[1, pl.ds(0, shared), :, :, pl.ds(0, comps)]
+    rest_sent = row_parts_x.at[pl.ds(0, n_lon - shared), :, :, pl.ds(0, comps)]
+    pl.when(edge_a)(lambda: wait_bytes(sent[0], send_b.at[0, 0]))
+    inside = jnp.logical_and(edge_a, jnp.logical_not(edge_b))
+    pl.when(inside)(lambda: wait_bytes(sent[1], send_b.at[1, 0]))
+    pl.when(jnp.logical_and(edge_a, edge_b))(lambda: wait_bytes(half_sent, send_b.at[1, 0]))
+    pl.when(helps)(lambda: wait_bytes(rest_sent, send_y))
+    for i in range(2):
+        pl.when(edge_b)(help_copy(i).wait_send)
 
 
 def solution(mesh):
@@ -498,6 +544,9 @@
                 pltpu.VMEM((2, n_lon, 2, levels, 8, cols), f32),
                 pltpu.VMEM((2, n_lon, levels, 8, cols), f32),
                 pltpu.VMEM((cols, cols), f32),
+                pltpu.VMEM((n_lat, 8, cols), f32),
+                pltpu.VMEM((levels, -(-n_lat * donor_cell.shape[3] // cols), 8, cols), f32),
+                pltpu.VMEM((n_lon, 2, levels, 8, cols), f32),
                 dma((4,)),
                 dma((2,)),
                 dma((2,)),
@@ -507,6 +556,9 @@
                 dma((2,)),
                 dma((2, 2)),
                 dma((2, 2)),
+                dma((2,)),
+                dma,
+                dma,
             ],
             compiler_params=pltpu.CompilerParams(
                 collective_id=0, has_side_effects=True, vmem_limit_bytes=32 * 2**20

time: 42.7 us -> 42.5 us (level)
  no operation moved by 1% of the time
where the time goes in v6:
time: 42.5 us; the launch traced here: 42.3 us
  Pallas kernels  41.6 us (98%)
  local copies, waits for them, and re-layouts  0.77 us (2%)
    pallas_call x1, Pallas kernels, per_device(): pl.pallas_call(functools.partial(kernel, n_lat, n_lon), out_shape=jax.Sha...  41.6 us

profile of v6, /device:TPU:1, one launch (start us, length us, event | category | flops | bytes accessed | tf_op | source)
XLA Modules:
  0.0 42.3 jit_solution(8948271099280874979)
XLA Ops:
  0.0 41.6 %shard_map.55 = f32[1,7,2,64,128]{4,3,2,1,0:T(8,128)S(1)} custom-call(f32[1,7,2,64,128]{4,3,2,1,0:T(8,128)} %state.1, s32[1,1,1,768]{3,2,1,0:T(1,128)} %slots.1, s32[1,1,1,48]{3,2,1,0:T(1,128)} %cell.1, f32[1,1,1,2,48]{4,3,2,1,0:T(2,128)} %frac.1, f32[1,1,1,48]{3,2,1,0:T(1,128)} %turn.1), custom_call_target="tpu_custom_call" | custom-call | tf_op jit(solution)/shard_map/pallas_call | solution.py:522
  41.6 0.8 %copy.7 = f32[1,7,2,64,128]{4,3,2,1,0:T(8,128)} copy(f32[1,7,2,64,128]{4,3,2,1,0:T(8,128)S(1)} %shard_map.55) | data formatting | bytes 917504

commit v7 on v6

--- a/solution.py
+++ b/solution.py
@@ -335,7 +335,6 @@
             total = jnp.sum(side_rim[s], axis=0)
 
             def put(side):
-                flip[...] = jnp.zeros_like(flip)
                 for level in range(levels):
                     both = (total[level], pltpu.roll(total[level], half, 1))
                     for t in range(2):
@@ -413,6 +412,8 @@
     def give(s):
         donate(s)
         if s == 0:
+            pack_sides(s)
+            pack_rows(s)
             pl.semaphore_wait(barrier, greeted)
         if s == 1:
             for i in range(2):
@@ -420,8 +421,9 @@
         start_a(s)
         if s == 0:
             send_slots()
-        pack_sides(s)
-        pack_rows(s)
+        if s == 1:
+            pack_sides(s)
+            pack_rows(s)
         start_halo(s)
 
     def mend_side(s):
@@ -462,6 +464,7 @@
         pl.when(first_a)(lambda: rates(s, emit, 0, 8))
         pl.when(last_a)(lambda: rates(s, emit, rows - 8, 8))
 
+    flip[...] = jnp.zeros_like(flip)
     for s in range(2):
 
         @pl.when(first_b)

time: 42.5 us -> 42.5 us (level)
  no operation moved by 1% of the time
where the time goes in v7:
time: 42.5 us; the launch traced here: 42.3 us
  Pallas kernels  41.6 us (98%)
  local copies, waits for them, and re-layouts  0.77 us (2%)
    pallas_call x1, Pallas kernels, per_device(): pl.pallas_call(functools.partial(kernel, n_lat, n_lon), out_shape=jax.Sha...  41.6 us

profile of v7, /device:TPU:1, one launch (start us, length us, event | category | flops | bytes accessed | tf_op | source)
XLA Modules:
  0.0 42.3 jit_solution(3952435046861291100)
XLA Ops:
  0.0 41.6 %shard_map.55 = f32[1,7,2,64,128]{4,3,2,1,0:T(8,128)S(1)} custom-call(f32[1,7,2,64,128]{4,3,2,1,0:T(8,128)} %state.1, s32[1,1,1,768]{3,2,1,0:T(1,128)} %slots.1, s32[1,1,1,48]{3,2,1,0:T(1,128)} %cell.1, f32[1,1,1,2,48]{4,3,2,1,0:T(2,128)} %frac.1, f32[1,1,1,48]{3,2,1,0:T(1,128)} %turn.1), custom_call_target="tpu_custom_call" | custom-call | tf_op jit(solution)/shard_map/pallas_call | solution.py:525
  41.6 0.8 %copy.7 = f32[1,7,2,64,128]{4,3,2,1,0:T(8,128)} copy(f32[1,7,2,64,128]{4,3,2,1,0:T(8,128)S(1)} %shard_map.55) | data formatting | bytes 917504
